TPU v7x, 512 devices: a whole 4x4x16 slice. The times are simulated.
512 devices in a mesh: pair: 32 (over z, core), aux: 16 (over x, y).
Axes of the slice: x: 4, y: 4, z: 16, core: 2. Of those that a mesh axis runs over, the one named last changes fastest.
Arguments:
- tiles: bfloat16 [5632, 64, 3328], P(('pair', 'aux')), may hold values from -6 to 6
- coeff: bfloat16 [4096, 256], P('pair'), may hold values from -0.375 to 0.375
- support: int32 [64, 48], P('pair'), may hold values from 0 to 255, all different within a row
- row_block: int32 [5632], P(('pair', 'aux')), may hold values from 0 to 1
- col_block: int32 [5632], P(('pair', 'aux')), may hold values from 0 to 63
- owner: int32 [5632, 1], P(('pair', 'aux')), may hold values from 0 to 15; in each aligned block of 11 rows (0 to 10, 11 to 21, ...) at most 2 rows name the same one
- local_block: int32 [5632], P(('pair', 'aux')), may hold values from 0 to 31
- metric: bfloat16 [512, 52, 52], P('aux'), may hold values from -0.015625 to 0.015625
Outputs:
- exchange: float32 [64, 64, 64], P('pair', 'aux')
Inputs may be any that keep to these rules, and one draw needn't show every extreme that they name: Within the 11 tiles of one device no owner appears more than 2 times; some device names one owner exactly 2 times. `support`: the 48 orbitals of one row are distinct; every orbital appears in some row.
All inputs are finite; a program needn't handle non-finite values.
Results may differ from a plain program's by a relative error of at most 0.0038.
Values may be sent and summed in bfloat16 or wider, within the bound.
No kernel may reach another device: no remote copies, remote signals or barrier semaphores. Data moves between devices by JAX's collectives and lax.ppermute only.
A program may use at most 64 MiB of HBM per device.

v0:
```python
import jax
import jax.numpy as jnp
from jax import lax
from jax.sharding import PartitionSpec as P


def slot_layout(owner_col, aux_count, slots_per):
    item_count = owner_col.shape[0]
    positions = jnp.arange(item_count, dtype=jnp.int32)
    earlier = (owner_col[:, None] == owner_col[None, :]) & (positions[None, :] < positions[:, None])
    rank_in_owner = jnp.sum(earlier.astype(jnp.int32), axis=1)
    slot_of = owner_col * slots_per + rank_in_owner
    slot_total = aux_count * slots_per
    matches = slot_of[None, :] == jnp.arange(slot_total, dtype=jnp.int32)[:, None]
    filled = jnp.any(matches, axis=1)
    item_of = jnp.sum(jnp.where(matches, positions[None, :], 0), axis=1)
    return (slot_of, filled, item_of)


def block_terms(halves, metric_tiles, block_width):
    item_count = halves.shape[0]
    shaped = halves.reshape(item_count, halves.shape[1], block_width, metric_tiles.shape[1])
    fitted = jnp.einsum(
        "csnp,cpq->csnq", shaped, metric_tiles, preferred_element_type=jnp.float32
    ).astype(jnp.bfloat16)
    return jnp.einsum("csnp,csmp->cnm", shaped, fitted, preferred_element_type=jnp.float32)


def dense_partial(targets, block_sums, block_total, block_width):
    onehot = (targets[:, None] == jnp.arange(block_total, dtype=jnp.int32)[None, :]).astype(
        jnp.float32
    )
    partial_value = -jnp.einsum("kb,kx->bx", onehot, block_sums, precision=lax.Precision.HIGHEST)
    return partial_value.reshape(block_total, block_width, block_width)


def shards(tiles, coeff, support, row_block, col_block, owner, local_block, metric):
    item_count = tiles.shape[0]
    block_width = tiles.shape[1]
    orbital_count = coeff.shape[1]
    blocks = coeff.shape[0] // block_width
    aux_count = lax.axis_size("aux")
    block_total = blocks * lax.axis_size("pair")
    slot_cap = max(2, -(-item_count // aux_count))
    coeff_rows = coeff.reshape(blocks, block_width, orbital_count)[row_block]
    picked = support[row_block]
    coeffs = jnp.take_along_axis(coeff_rows, picked[:, None, :], axis=2)
    halves = jnp.einsum("kms,kmx->ksx", coeffs, tiles, preferred_element_type=jnp.float32).astype(
        jnp.bfloat16
    )
    target_owner = owner[:, 0]
    slot_of, filled, item_of = slot_layout(target_owner, aux_count, slot_cap)
    wanted = jnp.where(filled, local_block[item_of], 0).reshape(aux_count, slot_cap)
    asked_blocks = lax.all_to_all(wanted, "aux", split_axis=0, concat_axis=0, tiled=True)
    served = metric[asked_blocks]
    returned = lax.all_to_all(served, "aux", split_axis=0, concat_axis=0, tiled=True)
    metric_tiles = returned.reshape(aux_count * slot_cap, returned.shape[2], returned.shape[3])[
        slot_of
    ]
    block_sums = block_terms(halves, metric_tiles, block_width).reshape(
        item_count, block_width * block_width
    )
    partial_value = dense_partial(col_block, block_sums, block_total, block_width)
    row_share = lax.psum_scatter(partial_value, "pair", scatter_dimension=0, tiled=True)
    result = lax.psum_scatter(row_share, "aux", scatter_dimension=1, tiled=True)
    return result


def solution(mesh):
    return jax.shard_map(
        shards,
        mesh=mesh,
        in_specs=(
            P(("pair", "aux"), None, None),
            P("pair", None),
            P("pair", None),
            P(("pair", "aux")),
            P(("pair", "aux")),
            P(("pair", "aux"), None),
            P(("pair", "aux")),
            P("aux", None, None),
        ),
        out_specs=P("pair", "aux", None),
        check_vma=False,
    )
```

profile of v0, /device:TPU:32, one launch (start us, length us, event | category | flops | bytes accessed | tf_op | source)
XLA Modules:
  0.0 285.2 jit_solution(4735378100731839565)
XLA Ops:
  6.5 0.0 copy-start
  6.5 0.9 convert_reduce_fusion
  7.4 0.7 multiply_add_fusion
  8.1 0.1 select_reduce_fusion
  8.2 0.1 fusion.15
  8.3 1.4 gather_fusion.2
  9.7 0.7 select_n.79
  10.4 7.0 %all-to-all-start = ((s32[16,1,2]{2,1,0:T(1,128)}), s32[16,1,2]{2,1,0:T(1,128)S(1)}, u32[]{:S(2)}, u32[]{:S(2)}) async-start(s32[16,1,2]{2,1,0:T(1,128)} %bitcast.6), calls=%async_computation | async-start | bytes 16384 | tf_op jit(solution)/shard_map/all_to_all | solution.py:54
  17.4 0.7 compare_select_fusion.5
  18.1 1.2 gather_fusion
  19.4 0.1 reshape.162
  19.4 1.4 gather_fusion.1
  20.8 0.4 copy.26
  21.2 7.0 %gather_fusion.5 = bf16[528,64]{1,0:T(8,128)(2,1)S(1)} fusion(bf16[11,64,256]{1,2,0:T(8,128)(2,1)S(1)} %copy.26, s32[528]{0:T(1024)S(1)} %reshape.162), kind=kCustom, calls=%fused_computation.5 | custom fusion | bytes 139392 | tf_op jit(solution)/shard_map/jit(take_along_axis)/gather | solution.py:47
  28.2 0.0 copy-start.2
  28.2 5.2 %convolution_convert_fusion = bf16[11,48,3328]{2,1,0:T(8,128)(2,1)} fusion(bf16[11,64,3328]{2,1,0:T(8,128)(2,1)} %param.8, bf16[11,48,64]{2,1,0:T(8,128)(2,1)S(1)} %bitcast.50, pred[11,48]{1,0:T(8,128)(4,1)S(1)} %compare_and_fusion), kind=kOutput, calls=%fused_computation.8 | convolution fusion | flops 226710528 | bytes 8268304 | tf_op jit(solution)/shard_map/kms,kmx->ksx/dot_general | solution.py:48
  33.5 0.0 all-to-all-done
  33.5 0.1 copy.28
  33.6 0.1 copy.29
  33.7 0.1 reshape.148
  33.8 0.0 copy-done
  33.8 2.2 gather_fusion.3
  36.0 0.3 copy.44
  36.3 1.3 reshape.176
  37.6 7.2 %all-to-all-start.1 = ((bf16[16,2,2704]{2,1,0:T(2,128)(2,1)}), bf16[16,2,2704]{2,1,0:T(2,128)(2,1)S(1)}, u32[]{:S(2)}, u32[]{:S(2)}) async-start(bf16[16,2,2704]{2,1,0:T(2,128)(2,1)} %reshape.176), calls=%async_computation.1 | async-start | bytes 360448 | tf_op jit(solution)/shard_map/all_to_all | solution.py:56
  44.8 0.2 reduce-scatter.3.cloned.1.call-start
  45.1 0.0 copy-done.2
  45.1 27.8 %reshape.118 = bf16[11,48,64,52]{3,2,1,0:T(8,128)(2,1)} reshape(bf16[11,48,3328]{2,1,0:T(8,128)(2,1)} %convolution_convert_fusion) | data formatting | bytes 7028736 | tf_op jit(solution)/shard_map/reshape | solution.py:22
  72.8 0.0 all-to-all-done.1
  72.9 0.7 reshape.177
  73.5 0.1 copy.31
  73.6 0.6 gather_fusion.4
  74.2 0.0 copy-start.1
  74.2 14.2 %fusion.4 = f32[11,64,64]{2,1,0:T(8,128)S(1)} fusion(bf16[11,48,64,52]{3,2,1,0:T(8,128)(2,1)} %reshape.118, bf16[11,52,52]{2,1,0:T(8,128)(2,1)S(1)} %gather_fusion.4), kind=kOutput, calls=%fused_computation.11 | convolution fusion | flops 409423872 | bytes 3754080 | tf_op jit(solution)/shard_map/csnp,csmp->cnm/dot_general | solution.py:26
  88.4 0.1 reshape.120
  88.6 0.0 copy-done.1
  88.6 0.7 convolution_negate_fusion
  89.3 2.2 reshape.121
  91.5 0.0 reduce-scatter.3.cloned.1.call-update
  91.5 1.3 dynamic-slice
  93.4 109.4 %reduce-scatter.3.cloned.1.call-done = f32[2,64,64]{2,1,0:T(8,128)} async-done(((f32[64,64,64]{2,1,0:T(8,128)}), f32[2,64,64]{2,1,0:T(8,128)}) %reduce-scatter.3.cloned.1.call-update) | async-done | bytes 32784 | tf_op jit(solution)/shard_map/reduce_scatter | solution.py:64
  202.8 75.0 %all-reduce = f32[2,64,64]{2,1,0:T(8,128)S(1)} all-reduce(f32[2,64,64]{2,1,0:T(8,128)} %reduce-scatter.3.cloned.1.call-done), channel_id=3, replica_groups=mesh['pair'=32,'aux'=16] {'aux'}, use_global_device_ids=true, to_apply=%region_4.5.clone | all-reduce | flops 8192 | bytes 65536
  277.8 0.6 constant_dynamic-slice_fusion
  (10 shorter events, 0.1 us)
Async XLA Ops:
  6.5 27.2 %copy-start = (bf16[32,52,52]{2,0,1:T(8,128)(2,1)S(1)}, bf16[32,52,52]{2,0,1:T(8,128)(2,1)}, u32[]{:S(2)}) copy-start(bf16[32,52,52]{2,0,1:T(8,128)(2,1)} %param.15) | copy-start | bytes 519172
  10.4 23.1 %all-to-all-start = ((s32[16,1,2]{2,1,0:T(1,128)}), s32[16,1,2]{2,1,0:T(1,128)S(1)}, u32[]{:S(2)}, u32[]{:S(2)}) async-start(s32[16,1,2]{2,1,0:T(1,128)} %bitcast.6), calls=%async_computation | async-start | bytes 16384 | tf_op jit(solution)/shard_map/all_to_all | solution.py:54
  28.2 16.8 %copy-start.2 = (s32[11,1]{0,1:T(1,128)S(1)}, s32[11,1]{0,1:T(1,128)}, u32[]{:S(2)}) copy-start(s32[11,1]{0,1:T(1,128)} %param.13) | copy-start | bytes 136
  37.6 35.2 %all-to-all-start.1 = ((bf16[16,2,2704]{2,1,0:T(2,128)(2,1)}), bf16[16,2,2704]{2,1,0:T(2,128)(2,1)S(1)}, u32[]{:S(2)}, u32[]{:S(2)}) async-start(bf16[16,2,2704]{2,1,0:T(2,128)(2,1)} %reshape.176), calls=%async_computation.1 | async-start | bytes 360448 | tf_op jit(solution)/shard_map/all_to_all | solution.py:56
  44.8 158.0 %reduce-scatter.3.cloned.1.call-start = ((), (), s32[]{:S(2)}) async-start(), calls=%async_computation.3 | async-start | bytes 2162688 | tf_op jit(solution)/shard_map/reduce_scatter | solution.py:64
  74.2 14.4 %copy-start.1 = (s32[11]{0:T(128)S(1)}, s32[11]{0:T(128)}, u32[]{:S(2)}) copy-start(s32[11]{0:T(128)} %param.12) | copy-start | bytes 136
Sparse Core Ops, SparseCore 0:
  91.6 111.1 reduce-scatter.2
where the time goes:
time: 286 us; the launch traced here: 285 us
  waiting for transfers between devices  109 us (38%)
  blocking collectives  75 us (26%)
  local copies, waits for them, and re-layouts  49.5 us (17%)
  matrix products  20.2 us (7%)
  starting transfers between devices  14.5 us (5%)
  between operations  14.2 us (5%)
    reduce_scatter x1, waiting for transfers between devices, shards(): lax.psum_scatter(partial_value, 'pair', scatter_dimension=0, tiled=True)  109 us
    unnamed x1, blocking collectives  75 us
    reshape x1, local copies, waits for them, and re-layouts, block_terms(): halves.reshape(item_count, halves.shape[1], block_width, metric_tiles.sha...  27.8 us
    dot_general x1, matrix products, block_terms(): jnp.einsum('csnp,csmp->cnm', shaped, fitted, preferred_element_type=jnp.f...  14.2 us
    all_to_all x1, starting transfers between devices, shards(): lax.all_to_all(served, 'aux', split_axis=0, concat_axis=0, tiled=True)  7.22 us
    gather x2, local copies, waits for them, and re-layouts, shards(): coeffs = jnp.take_along_axis(coeff_rows, picked[:, None, :], axis=2)  7.06 us
    all_to_all x1, starting transfers between devices, shards(): lax.all_to_all(wanted, 'aux', split_axis=0, concat_axis=0, tiled=True)  7.03 us
  transfers between devices with their start and end apart: 3, of which 1 were waited for; matrix products, arithmetic and copies ran while one was open for 16% of the time, Pallas kernels for 0%

commit v1 on v0

v1 whole, which is shorter than its diff:
```python
import functools
import jax
import jax.numpy as jnp
from jax import lax
from jax.experimental import pallas as pl
from jax.experimental.pallas import tpu as pltpu
from jax.sharding import PartitionSpec as P

LANES = 128
HALF = 64
SLOTS = 8


def request_kernel(owner_ref, local_ref, col_ref, out_ref):
    aux_count = out_ref.shape[0]
    shape = (aux_count, owner_ref.shape[1])
    position = lax.broadcasted_iota(jnp.int32, shape, 1)
    match = owner_ref[...] == lax.broadcasted_iota(jnp.int32, shape, 0)
    local = jnp.broadcast_to(local_ref[...], shape)
    first = jnp.min(jnp.where(match, position, LANES), axis=1, keepdims=True)
    last = jnp.max(jnp.where(match, position, -1), axis=1, keepdims=True)
    out_ref[...] = jnp.zeros_like(out_ref)
    out_ref[:, 0:1] = jnp.sum(jnp.where(position == first, local, 0), axis=1, keepdims=True)
    out_ref[:, 1:2] = jnp.sum(jnp.where(position == last, local, 0), axis=1, keepdims=True)
    out_ref[:, 32 : 32 + shape[1]] = jnp.broadcast_to(col_ref[...], shape)


def half_kernel(row_ref, tile_ref, coeff_ref, support_ref, out_ref, picked, half, slabs):
    width = tile_ref.shape[1]
    orbitals = support_ref.shape[1]
    groups = orbitals // 2
    aux_width = tile_ref.shape[2] // width

    @pl.when(pl.program_id(0) == 0)
    def _():
        for block in range(support_ref.shape[0]):
            shape = (coeff_ref.shape[1], orbitals)
            onehot = support_ref[block : block + 1, :] == lax.broadcasted_iota(jnp.int32, shape, 0)
            chosen = jnp.dot(
                coeff_ref[block * width : (block + 1) * width, :],
                onehot.astype(jnp.float32).astype(jnp.bfloat16),
                preferred_element_type=jnp.float32,
            )
            picked[block] = chosen.T.astype(jnp.bfloat16)

    half[...] = jnp.dot(
        picked[row_ref[pl.program_id(0)]], tile_ref[0], preferred_element_type=jnp.float32
    )
    lane = lax.broadcasted_iota(jnp.int32, (orbitals, LANES), 1)
    low = lane[:groups] < HALF
    for nu in range(width):
        start = nu * aux_width
        base, shift = start // LANES * LANES, start % LANES
        window = half[:, base : base + LANES]
        if shift + aux_width > LANES:
            window = jnp.where(lane >= shift, window, half[:, base + LANES : base + 2 * LANES])
        first, second = window[:groups], window[groups:]
        if shift:
            first = pltpu.roll(first, LANES - shift, 1)
        if shift != HALF:
            second = pltpu.roll(second, (LANES + HALF - shift) % LANES, 1)
        slabs[nu * groups : (nu + 1) * groups, :] = jnp.where(low, first, second)
    for g in range(groups):
        out_ref[0, g * width : (g + 1) * width, :] = slabs[
            pl.ds(g, width, stride=groups), :
        ].astype(jnp.bfloat16)


def serve_kernel(asked_ref, metric_ref, out_ref):
    lane = lax.broadcasted_iota(jnp.int32, out_ref.shape[1:], 1)
    for peer in range(out_ref.shape[0]):
        out_ref[peer] = jnp.where(
            lane < HALF, metric_ref[asked_ref[peer, 0]], metric_ref[asked_ref[peer, 1]]
        )


def term_kernel(owner_ref, first_ref, second_ref, metric_ref, out_ref, total):
    pair = pl.program_id(0)
    item_count = owner_ref.shape[0]
    width = metric_ref.shape[1]
    groups = first_ref.shape[1] // width
    lane = lax.broadcasted_iota(jnp.int32, (width, LANES), 1)

    def placed(item):
        mine = owner_ref[item]
        slot = jnp.int32(0)
        for other in range(item_count):
            slot = slot | jnp.where((owner_ref[other] == mine) & (other < item), 1, 0)
        block = metric_ref[mine].astype(jnp.float32)
        turned = pltpu.roll(block, HALF, 1)
        low = jnp.where(slot == 0, block, turned)
        high = jnp.where(slot == 0, turned, block)
        stacked = [jnp.where(lane < HALF, low, 0.0), jnp.where(lane < HALF, 0.0, high)]
        return jnp.concatenate(stacked, axis=0).astype(jnp.bfloat16)

    @pl.when(pair == 0)
    def _():
        total[...] = jnp.zeros_like(total)

    gap = item_count - pl.num_programs(0)
    metric_a, metric_b = placed(pair), placed(pair + gap)
    zero = jnp.zeros_like(metric_a)
    metrics = jnp.concatenate(
        [jnp.concatenate([metric_a, zero], axis=1), jnp.concatenate([zero, metric_b], axis=1)],
        axis=0,
    )
    halves = jnp.concatenate([first_ref[0], second_ref[0]], axis=1)
    fitted = jnp.dot(halves, metrics, preferred_element_type=jnp.float32).astype(jnp.bfloat16)

    def spread(array):
        rows = [
            jnp.concatenate(
                [
                    array[g * width : (g + 1) * width, side * LANES : (side + 1) * LANES]
                    for g in range(groups)
                ],
                axis=1,
            )
            for side in range(2)
        ]
        return jnp.concatenate(rows, axis=0)

    product = lax.dot_general(
        spread(halves),
        spread(fitted),
        (((1,), (1,)), ((), ())),
        preferred_element_type=jnp.float32,
    )
    total[pl.ds(pair, width, stride=SLOTS), :] = jnp.where(
        lane < HALF, product[:width], product[width:]
    )

    @pl.when(pair == pl.num_programs(0) - 1)
    def _():
        out_ref[...] = total[...].astype(jnp.bfloat16)


def combine_kernel(parts_ref, pick_ref, out_ref):
    sources = parts_ref.shape[0]
    rows = parts_ref.shape[1] // SLOTS
    pairs = pick_ref.shape[0] // 8
    low = lax.broadcasted_iota(jnp.int32, (pairs, LANES), 1) < HALF
    for step in range(rows // 2):
        block = parts_ref[:, step * 2 * SLOTS : (step + 1) * 2 * SLOTS, :]
        summed = jnp.dot(
            pick_ref[...],
            block.reshape(sources * 2 * SLOTS, LANES),
            preferred_element_type=jnp.float32,
        )
        for parity in range(2):
            at = parity * 4 * pairs
            even = summed[at : at + pairs] + pltpu.roll(summed[at + pairs : at + 2 * pairs], HALF, 1)
            odd = summed[at + 3 * pairs : at + 4 * pairs] + pltpu.roll(
                summed[at + 2 * pairs : at + 3 * pairs], HALF, 1
            )
            out_ref[pl.ds(step * 2 + parity, pairs, stride=rows), :] = jnp.where(low, even, odd)


def final_kernel(parts_ref, out_ref):
    rows = out_ref.shape[1]
    summed = jnp.sum(parts_ref[...], axis=0)
    for side in range(out_ref.shape[0]):
        out_ref[side] = summed[:, side * HALF : (side + 1) * HALF]


def shards(tiles, coeff, support, row_block, col_block, owner, local_block, metric):
    item_count, width, columns = tiles.shape
    aux_width = metric.shape[1]
    orbitals = support.shape[1]
    aux_count = lax.axis_size("aux")
    pair_count = lax.axis_size("pair")
    groups = orbitals // 2
    pair_steps = (item_count + 1) // 2
    gap = item_count - pair_steps
    vmem = pl.BlockSpec(memory_space=pltpu.VMEM)
    smem = pl.BlockSpec(memory_space=pltpu.SMEM)
    row = lambda array: array.reshape(1, item_count)

    request = pl.pallas_call(
        request_kernel,
        out_shape=jax.ShapeDtypeStruct((aux_count, LANES), jnp.int32),
        in_specs=[vmem] * 3,
        out_specs=vmem,
        name="request",
    )(row(owner), row(local_block), row(col_block))
    asked = lax.all_to_all(
        request.reshape(aux_count, 1, LANES), "aux", split_axis=0, concat_axis=0, tiled=True
    ).reshape(aux_count, LANES)

    halves = pl.pallas_call(
        half_kernel,
        grid_spec=pltpu.PrefetchScalarGridSpec(
            num_scalar_prefetch=1,
            grid=(item_count,),
            in_specs=[
                pl.BlockSpec((1, width, columns), lambda k, rows: (k, 0, 0)),
                pl.BlockSpec(coeff.shape, lambda k, rows: (0, 0)),
                pl.BlockSpec(support.shape, lambda k, rows: (0, 0)),
            ],
            out_specs=pl.BlockSpec((1, groups * width, LANES), lambda k, rows: (k, 0, 0)),
            scratch_shapes=[
                pltpu.VMEM((support.shape[0], orbitals, width), jnp.bfloat16),
                pltpu.VMEM((orbitals, columns), jnp.float32),
                pltpu.VMEM((groups * width, LANES), jnp.float32),
            ],
        ),
        out_shape=jax.ShapeDtypeStruct((item_count, groups * width, LANES), jnp.bfloat16),
        cost_estimate=pl.CostEstimate(
            flops=2 * item_count * orbitals * width * columns,
            bytes_accessed=2 * item_count * (width * columns + groups * width * LANES),
            transcendentals=0,
        ),
        name="half",
    )(row_block, tiles, coeff, support)

    side = jnp.pad(metric, ((0, 0), (0, width - aux_width), (0, HALF - aux_width)))
    padded = jnp.concatenate([side, side], axis=2)
    served = pl.pallas_call(
        serve_kernel,
        out_shape=jax.ShapeDtypeStruct((aux_count, width, LANES), jnp.bfloat16),
        in_specs=[smem, vmem],
        out_specs=vmem,
        name="serve",
    )(asked, padded)
    metric_tiles = lax.all_to_all(served, "aux", split_axis=0, concat_axis=0, tiled=True)

    cols = asked[:, 32 : 32 + item_count]
    fill = ((0, 0), (0, SLOTS - pair_steps))
    cols_a = jnp.pad(cols[:, :pair_steps], fill, constant_values=-1)
    cols_b = jnp.pad(cols[:, gap:], fill, constant_values=-1)
    cols_b = jnp.where(jnp.arange(SLOTS)[None, :] < pair_steps - gap, -1, cols_b)
    spread = lambda array: jnp.broadcast_to(array[:, None, :], (aux_count, 2, SLOTS)).reshape(1, -1)
    place = jnp.arange(8 * pair_count, dtype=jnp.int32)[:, None]
    block = 2 * (place % pair_count) + place // (2 * pair_count) % 2
    side_b = place // pair_count % 2 == 1
    parity = jnp.arange(aux_count * 2 * SLOTS, dtype=jnp.int32)[None, :] // SLOTS % 2
    hit = jnp.where(side_b, spread(cols_b) == block, spread(cols_a) == block)
    pick = jnp.where(hit & (parity == place // (4 * pair_count)), -1.0, 0.0).astype(jnp.bfloat16)

    blocks = pl.pallas_call(
        term_kernel,
        grid_spec=pltpu.PrefetchScalarGridSpec(
            num_scalar_prefetch=1,
            grid=(pair_steps,),
            in_specs=[
                pl.BlockSpec((1, groups * width, LANES), lambda t, own: (t, 0, 0)),
                pl.BlockSpec((1, groups * width, LANES), lambda t, own: (t + gap, 0, 0)),
                pl.BlockSpec((aux_count, width, LANES), lambda t, own: (0, 0, 0)),
            ],
            out_specs=pl.BlockSpec((width * SLOTS, LANES), lambda t, own: (0, 0)),
            scratch_shapes=[pltpu.VMEM((width * SLOTS, LANES), jnp.float32)],
        ),
        out_shape=jax.ShapeDtypeStruct((width * SLOTS, LANES), jnp.bfloat16),
        compiler_params=pltpu.CompilerParams(vmem_limit_bytes=32 * 1024 * 1024),
        name="term",
    )(owner.reshape(item_count), halves, halves, metric_tiles)
    rows = width // aux_count
    parts = lax.all_to_all(
        blocks.reshape(aux_count, rows * SLOTS, LANES), "aux", split_axis=0, concat_axis=0, tiled=True
    )

    sums = pl.pallas_call(
        combine_kernel,
        out_shape=jax.ShapeDtypeStruct((pair_count * rows, LANES), jnp.float32),
        in_specs=[vmem] * 2,
        out_specs=vmem,
        name="combine",
    )(parts, pick)
    arrived = lax.all_to_all(
        sums.reshape(pair_count, rows, LANES), "pair", split_axis=0, concat_axis=0, tiled=True
    )
    return pl.pallas_call(
        final_kernel,
        out_shape=jax.ShapeDtypeStruct((2, rows, width), jnp.float32),
        in_specs=[vmem],
        out_specs=vmem,
        name="final",
    )(arrived)


def solution(mesh):
    return jax.shard_map(
        shards,
        mesh=mesh,
        in_specs=(
            P(("pair", "aux"), None, None),
            P("pair", None),
            P("pair", None),
            P(("pair", "aux")),
            P(("pair", "aux")),
            P(("pair", "aux"), None),
            P(("pair", "aux")),
            P("aux", None, None),
        ),
        out_specs=P("pair", "aux", None),
        check_vma=False,
    )
```

time: 286 us -> 96.4 us (0.34)
  the two profiles are of different devices: /device:TPU:32 before, /device:TPU:1 now
where the time goes in v1:
time: 96.4 us; the launch traced here: 95.6 us
  blocking collectives  32.5 us (34%)
  Pallas kernels  25.5 us (26%)
  starting transfers between devices  17.7 us (18%)
  waiting for transfers between devices  12.1 us (13%)
  local copies, waits for them, and re-layouts  5.85 us (6%)
  other arithmetic  1.93 us (2%)
    all_to_all x1, blocking collectives, shards(): lax.all_to_all(sums.reshape(pair_count, rows, LANES), 'pair', split_axis=...  32.5 us
    pallas_call x1, Pallas kernels, shards(): pl.pallas_call(half_kernel, grid_spec=pltpu.PrefetchScalarGridSpec(num_sc...  12.6 us
    all_to_all x1, starting transfers between devices, shards(): lax.all_to_all(request.reshape(aux_count, 1, LANES), 'aux', split_axis=0,...  7.58 us
    all_to_all x1, starting transfers between devices, shards(): lax.all_to_all(served, 'aux', split_axis=0, concat_axis=0, tiled=True)  6.65 us
    all_to_all x1, waiting for transfers between devices, shards(): lax.all_to_all(served, 'aux', split_axis=0, concat_axis=0, tiled=True)  6.23 us
    pallas_call x1, Pallas kernels, shards(): pl.pallas_call(term_kernel, grid_spec=pltpu.PrefetchScalarGridSpec(num_sc...  6.1 us
    all_to_all x1, waiting for transfers between devices, shards(): lax.all_to_all(blocks.reshape(aux_count, rows * SLOTS, LANES), 'aux', spl...  5.82 us
    unnamed x9, local copies, waits for them, and re-layouts  4.65 us
  transfers between devices with their start and end apart: 3, of which 2 were waited for; matrix products, arithmetic and copies ran while one was open for 5% of the time, Pallas kernels for 13%

profile of v1, /device:TPU:1, one launch (start us, length us, event | category | flops | bytes accessed | tf_op | source)
XLA Modules:
  0.0 95.6 jit_solution(16239608807235330767)
XLA Ops:
  0.0 1.5 %request.1 = s32[16,128]{1,0:T(8,128)} custom-call(s32[1,11]{1,0:T(1,128)} %bitcast.10, s32[1,11]{1,0:T(1,128)} %bitcast.16, s32[1,11]{1,0:T(1,128)} %bitcast.17), custom_call_target="tpu_custom_call" | custom-call | tf_op jit(solution)/shard_map/request/pallas_call | solution.py:179
  1.5 7.6 %all-to-all-start = ((s32[16,1,128]{2,1,0:T(1,128)}), s32[16,1,128]{2,1,0:T(1,128)S(1)}, u32[]{:S(2)}, u32[]{:S(2)}) async-start(s32[16,1,128]{2,1,0:T(1,128)} %bitcast.15), calls=%async_computation | async-start | bytes 16384 | tf_op jit(solution)/shard_map/all_to_all | solution.py:186
  9.2 1.2 %copy.12 = bf16[32,52,52]{2,1,0:T(8,128)(2,1)S(1)} copy(bf16[32,52,52]{2,0,1:T(8,128)(2,1)} %param.15) | data formatting | bytes 346112 | tf_op args[7]
  10.4 0.1 pad.11
  10.5 1.1 %pad_maximum_fusion.metric_ref = bf16[32,64,128]{2,1,0:T(8,128)(2,1)} fusion(bf16[32,64,64]{2,1,0:T(8,128)(2,1)S(1)} %pad.11), kind=kLoop, calls=%fused_computation | loop fusion | flops 1048576 | bytes 786432 | tf_op jit(solution)/shard_map/concatenate | solution.py:217
  11.6 0.0 copy-start.1
  11.6 12.6 %half.1.first_ref.second_ref = bf16[11,1536,128]{2,1,0:T(8,128)(2,1)} custom-call(s32[11]{0:T(128)} %row_ref.1, bf16[11,64,3328]{2,1,0:T(8,128)(2,1)} %tile_ref.1, bf16[128,256]{1,0:T(8,128)(2,1)} %coeff_ref.1, s32[2,48]{1,0:T(2,128)} %support_ref.1), custom_call_target="tpu_custom_call" | custom-call | flops 224919552 | bytes 9011200 | tf_op jit(solution)/shard_map/half/pallas_call | solution.py:190
  24.2 0.0 all-to-all-done
  24.2 0.0 copy-start.3
  24.2 0.6 copy-done.3
  24.8 1.8 %serve.1 = bf16[16,64,128]{2,1,0:T(8,128)(2,1)} custom-call(s32[16,128]{1,0:T(8,128)} %bitcast.13, bf16[32,64,128]{2,1,0:T(8,128)(2,1)} %pad_maximum_fusion.metric_ref), custom_call_target="tpu_custom_call" | custom-call | tf_op jit(solution)/shard_map/serve/pallas_call | solution.py:218
  26.6 6.7 %all-to-all-start.1 = ((bf16[16,64,128]{2,1,0:T(8,128)(2,1)}), bf16[16,64,128]{2,1,0:T(8,128)(2,1)S(1)}, u32[]{:S(2)}, u32[]{:S(2)}) async-start(bf16[16,64,128]{2,1,0:T(8,128)(2,1)} %serve.1), calls=%async_computation.1 | async-start | bytes 524288 | tf_op jit(solution)/shard_map/all_to_all | solution.py:225
  33.3 0.8 fusion.9
  34.2 0.1 eq.59
  34.3 0.1 eq.63
  34.4 6.2 %all-to-all-done.1.metric_ref = bf16[16,64,128]{2,1,0:T(8,128)(2,1)S(1)} async-done(((bf16[16,64,128]{2,1,0:T(8,128)(2,1)}), bf16[16,64,128]{2,1,0:T(8,128)(2,1)S(1)}, u32[]{:S(2)}, u32[]{:S(2)}) %all-to-all-start.1) | async-done | bytes 262176 | tf_op jit(solution)/shard_map/all_to_all | solution.py:225
  40.6 0.0 copy-done.1
  40.6 0.0 copy-start
  40.6 2.2 %copy-done = bf16[11,1536,128]{2,1,0:T(8,128)(2,1)S(1)} copy-done((bf16[11,1536,128]{2,1,0:T(8,128)(2,1)S(1)}, bf16[11,1536,128]{2,1,0:T(8,128)(2,1)}, u32[]{:S(2)}) %copy-start) | copy-done | bytes 4325400
  42.8 6.1 %term.1 = bf16[512,128]{1,0:T(8,128)(2,1)} custom-call(s32[11]{0:T(128)S(1)} %bitcast.11, bf16[11,1536,128]{2,1,0:T(8,128)(2,1)S(1)} %copy-done, bf16[11,1536,128]{2,1,0:T(8,128)(2,1)S(1)} %copy-done, bf16[16,64,128]{2,1,0:T(8,128)(2,1)S(1)} %all-to-all-done.1.metric_ref), custom_call_target="tpu_custom_call" | custom-call | tf_op jit(solution)/shard_map/term/pallas_call | solution.py:240
  49.0 3.5 %all-to-all-start.2 = ((bf16[16,32,128]{2,1,0:T(8,128)(2,1)}), bf16[16,32,128]{2,1,0:T(8,128)(2,1)S(1)}, u32[]{:S(2)}, u32[]{:S(2)}) async-start(bf16[16,32,128]{2,1,0:T(8,128)(2,1)} %bitcast.7), calls=%async_computation.2 | async-start | bytes 262144 | tf_op jit(solution)/shard_map/all_to_all | solution.py:258
  52.5 0.8 select_convert_fusion.pick_ref
  53.3 5.8 %all-to-all-done.2.parts_ref = bf16[16,32,128]{2,1,0:T(8,128)(2,1)S(1)} async-done(((bf16[16,32,128]{2,1,0:T(8,128)(2,1)}), bf16[16,32,128]{2,1,0:T(8,128)(2,1)S(1)}, u32[]{:S(2)}, u32[]{:S(2)}) %all-to-all-start.2) | async-done | bytes 131104 | tf_op jit(solution)/shard_map/all_to_all | solution.py:258
  59.1 0.0 copy-start.2
  59.1 0.7 copy-done.2
  59.8 1.9 %combine.1 = f32[128,128]{1,0:T(8,128)} custom-call(bf16[16,32,128]{2,1,0:T(8,128)(2,1)} %copy-done.2, bf16[256,256]{1,0:T(8,128)(2,1)} %select_convert_fusion.pick_ref), custom_call_target="tpu_custom_call" | custom-call | tf_op jit(solution)/shard_map/combine/pallas_call | solution.py:262
  61.6 32.5 %all_to_all.20.parts_ref = f32[32,4,128]{2,1,0:T(4,128)} all-to-all(f32[32,4,128]{2,1,0:T(4,128)} %bitcast.12), channel_id=1, replica_groups=mesh['pair'=32,'aux'=16] {'pair'}, dimensions={0} | all-to-all | bytes 131072 | tf_op jit(solution)/shard_map/all_to_all | solution.py:269
  94.1 1.5 %final.1 = f32[2,4,64]{2,1,0:T(4,128)} custom-call(f32[32,4,128]{2,1,0:T(4,128)} %all_to_all.20.parts_ref), custom_call_target="tpu_custom_call" | custom-call | tf_op jit(solution)/shard_map/final/pallas_call | solution.py:272
  (8 shorter events, 0.1 us)
Async XLA Ops:
  1.5 22.7 %all-to-all-start = ((s32[16,1,128]{2,1,0:T(1,128)}), s32[16,1,128]{2,1,0:T(1,128)S(1)}, u32[]{:S(2)}, u32[]{:S(2)}) async-start(s32[16,1,128]{2,1,0:T(1,128)} %bitcast.15), calls=%async_computation | async-start | bytes 16384 | tf_op jit(solution)/shard_map/all_to_all | solution.py:186
  11.6 29.0 %copy-start.1 = (s32[11,1]{0,1:T(1,128)S(1)}, s32[11,1]{0,1:T(1,128)}, u32[]{:S(2)}) copy-start(s32[11,1]{0,1:T(1,128)} %param.13) | copy-start | bytes 136
  24.2 0.6 copy-start.3
  26.6 14.0 %all-to-all-start.1 = ((bf16[16,64,128]{2,1,0:T(8,128)(2,1)}), bf16[16,64,128]{2,1,0:T(8,128)(2,1)S(1)}, u32[]{:S(2)}, u32[]{:S(2)}) async-start(bf16[16,64,128]{2,1,0:T(8,128)(2,1)} %serve.1), calls=%async_computation.1 | async-start | bytes 524288 | tf_op jit(solution)/shard_map/all_to_all | solution.py:225
  40.6 2.2 %copy-start = (bf16[11,1536,128]{2,1,0:T(8,128)(2,1)S(1)}, bf16[11,1536,128]{2,1,0:T(8,128)(2,1)}, u32[]{:S(2)}) copy-start(bf16[11,1536,128]{2,1,0:T(8,128)(2,1)} %half.1.first_ref.second_ref) | copy-start | bytes 12976132
  49.0 10.1 %all-to-all-start.2 = ((bf16[16,32,128]{2,1,0:T(8,128)(2,1)}), bf16[16,32,128]{2,1,0:T(8,128)(2,1)S(1)}, u32[]{:S(2)}, u32[]{:S(2)}) async-start(bf16[16,32,128]{2,1,0:T(8,128)(2,1)} %bitcast.7), calls=%async_computation.2 | async-start | bytes 262144 | tf_op jit(solution)/shard_map/all_to_all | solution.py:258
  59.1 0.7 copy-start.2

commit v2 on v1

v2 whole, which is shorter than its diff:
```python
import jax
import jax.numpy as jnp
from jax import lax
from jax.experimental import pallas as pl
from jax.experimental.pallas import tpu as pltpu
from jax.sharding import PartitionSpec as P

LANES = 128
HALF = 64
MIB = 1 << 20
EARLY_LIMIT = 61_000_000
SERVE_LIMIT = 55_700_000
LATE_LIMIT = 51_000_000
TERM_LIMIT = 51_000_000
SLOTS = 8


def request_kernel(owner_ref, local_ref, col_ref, out_ref):
    aux_count = out_ref.shape[0]
    shape = (aux_count, owner_ref.shape[1])
    position = lax.broadcasted_iota(jnp.int32, shape, 1)
    match = owner_ref[...] == lax.broadcasted_iota(jnp.int32, shape, 0)
    local = jnp.broadcast_to(local_ref[...], shape)
    first = jnp.min(jnp.where(match, position, LANES), axis=1, keepdims=True)
    last = jnp.max(jnp.where(match, position, -1), axis=1, keepdims=True)
    out_ref[...] = jnp.zeros_like(out_ref)
    out_ref[:, 0:1] = jnp.sum(jnp.where(position == first, local, 0), axis=1, keepdims=True)
    out_ref[:, 1:2] = jnp.sum(jnp.where(position == last, local, 0), axis=1, keepdims=True)
    out_ref[:, 32 : 32 + shape[1]] = jnp.broadcast_to(col_ref[...], shape)


def place(metric_ref, coeff_ref, support_ref, padded_ref, picked_ref, rows_ref):
    aux_width, blocks, _ = metric_ref.shape
    width = coeff_ref.shape[0] // support_ref.shape[0]
    shape = (coeff_ref.shape[1], support_ref.shape[1])
    for block in range(support_ref.shape[0]):
        onehot = support_ref[block : block + 1, :] == lax.broadcasted_iota(jnp.int32, shape, 0)
        chosen = jnp.dot(
            coeff_ref[block * width : (block + 1) * width, :],
            onehot.astype(jnp.float32).astype(jnp.bfloat16),
            preferred_element_type=jnp.float32,
        )
        picked_ref[block] = chosen.T.astype(jnp.bfloat16)
    rows_ref[...] = jnp.zeros_like(rows_ref)
    for p in range(aux_width):
        rows_ref[p * blocks : (p + 1) * blocks, :aux_width] = metric_ref[p].astype(jnp.float32)
    padded_ref[...] = jnp.zeros_like(padded_ref)
    for block in range(blocks):
        entry = rows_ref[pl.ds(block, aux_width, stride=blocks), :]
        padded_ref[block, :aux_width, :] = (entry + pltpu.roll(entry, HALF, 1)).astype(jnp.bfloat16)


def fetch(tile_ref, first, buffer_ref, sems):
    copies = [
        pltpu.make_async_copy(tile_ref.at[first + item], buffer_ref.at[item], sems.at[item])
        for item in range(buffer_ref.shape[0])
    ]
    for copy in copies:
        copy.start()
    return copies


def half_tiles(row_ref, first, picked_ref, copies, buffer_ref, half_ref, slab_ref, put):
    item_count, width, columns = buffer_ref.shape
    orbitals = picked_ref.shape[1]
    groups = orbitals // 2
    aux_width = columns // width
    lane = lax.broadcasted_iota(jnp.int32, (orbitals, LANES), 1)
    low = lane[:groups] < HALF

    def multiply(item):
        copies[item].wait()
        half_ref[item % 2] = jnp.dot(
            picked_ref[row_ref[first + item]], buffer_ref[item], preferred_element_type=jnp.float32
        )

    multiply(0)
    for item in range(item_count):
        if item + 1 < item_count:
            multiply(item + 1)
        half, slabs = half_ref.at[item % 2], slab_ref.at[item % 2]
        for nu in range(width):
            start = nu * aux_width
            base, shift = start // LANES * LANES, start % LANES
            window = half[:, base : base + LANES]
            if shift + aux_width > LANES:
                window = jnp.where(lane >= shift, window, half[:, base + LANES : base + 2 * LANES])
            front, back = window[:groups], window[groups:]
            if shift:
                front = pltpu.roll(front, LANES - shift, 1)
            if shift != HALF:
                back = pltpu.roll(back, (LANES + HALF - shift) % LANES, 1)
            slabs[nu * groups : (nu + 1) * groups, :] = jnp.where(low, front, back)
        for g in range(groups):
            put(item, g * width, slabs[pl.ds(g, width, stride=groups), :].astype(jnp.bfloat16))


def early_kernel(row_ref, tile_ref, metric_ref, coeff_ref, support_ref, *refs):
    out_ref, padded_ref, picked_ref, rows_ref, made_ref, buffer_ref, half_ref, slab_ref, sems = refs
    count = buffer_ref.shape[0]
    first = tile_ref.shape[0] - count
    copies = fetch(tile_ref, first, buffer_ref, sems)
    place(metric_ref, coeff_ref, support_ref, padded_ref, picked_ref, rows_ref)
    sends = [
        pltpu.make_async_copy(made_ref.at[item], out_ref.at[item], sems.at[count + item])
        for item in range(count)
    ]

    def put(item, at, rows):
        made_ref[item, at : at + rows.shape[0], :] = rows
        if at + rows.shape[0] == made_ref.shape[1]:
            sends[item].start()

    half_tiles(row_ref, first, picked_ref, copies, buffer_ref, half_ref, slab_ref, put)
    for send in sends:
        send.wait()


def late_kernel(row_ref, tile_ref, picked_ref, out_ref, buffer_ref, half_ref, slab_ref, sems):
    copies = fetch(tile_ref, 0, buffer_ref, sems)

    def put(item, at, rows):
        out_ref[item, at : at + rows.shape[0], :] = rows

    half_tiles(row_ref, 0, picked_ref, copies, buffer_ref, half_ref, slab_ref, put)


def serve_kernel(asked_ref, metric_ref, out_ref):
    lane = lax.broadcasted_iota(jnp.int32, out_ref.shape[1:], 1)
    for peer in range(out_ref.shape[0]):
        out_ref[peer] = jnp.where(
            lane < HALF, metric_ref[asked_ref[peer, 0]], metric_ref[asked_ref[peer, 1]]
        )


def term_kernel(owner_ref, late_ref, early_ref, metric_ref, out_ref, total):
    late_count, rows, _ = late_ref.shape
    item_count = late_count + early_ref.shape[0]
    width = out_ref.shape[0] // SLOTS
    depth = metric_ref.shape[1]
    steps = (item_count + 1) // 2
    gap = item_count - steps
    groups = rows // width
    lane = lax.broadcasted_iota(jnp.int32, (depth, LANES), 1)
    rest = jnp.zeros((HALF - depth, LANES), jnp.float32)

    def placed(item):
        mine = owner_ref[item]
        slot = jnp.int32(0)
        for other in range(item):
            slot = slot | jnp.where(owner_ref[other] == mine, 1, 0)
        block = metric_ref[mine].astype(jnp.float32)
        turned = pltpu.roll(block, HALF, 1)
        low = jnp.where(slot == 0, block, turned)
        high = jnp.where(slot == 0, turned, block)
        stacked = [jnp.where(lane < HALF, low, 0.0), rest, jnp.where(lane < HALF, 0.0, high), rest]
        return jnp.concatenate(stacked, axis=0).astype(jnp.bfloat16)

    def spread(array):
        return jnp.concatenate(
            [array[g * width : (g + 1) * width, :] for g in range(groups)], axis=1
        )

    def term(item):
        halves = late_ref[item] if item < late_count else early_ref[item - late_count]
        fitted = jnp.dot(halves, placed(item), preferred_element_type=jnp.float32)
        return lax.dot_general(
            spread(halves),
            spread(fitted.astype(jnp.bfloat16)),
            (((1,), (1,)), ((), ())),
            preferred_element_type=jnp.float32,
        )

    total[...] = jnp.zeros_like(total)
    terms = []
    for item in range(item_count):
        terms.append(term(item))
        if item >= gap and item - gap < steps:
            at = item - gap
            total[pl.ds(at, width, stride=SLOTS), :] = jnp.concatenate(
                [terms[at], terms[item]], axis=1
            )
    out_ref[...] = total[...].astype(jnp.bfloat16)


def combine_kernel(parts_ref, pick_ref, out_ref):
    sources = parts_ref.shape[0]
    rows = parts_ref.shape[1] // SLOTS
    pairs = pick_ref.shape[0] // 8
    low = lax.broadcasted_iota(jnp.int32, (pairs, LANES), 1) < HALF
    for step in range(rows // 2):
        block = parts_ref[:, step * 2 * SLOTS : (step + 1) * 2 * SLOTS, :]
        summed = jnp.dot(
            pick_ref[...],
            block.reshape(sources * 2 * SLOTS, LANES),
            preferred_element_type=jnp.float32,
        )
        for parity in range(2):
            at = parity * 4 * pairs
            even = summed[at : at + pairs] + pltpu.roll(summed[at + pairs : at + 2 * pairs], HALF, 1)
            odd = summed[at + 3 * pairs : at + 4 * pairs] + pltpu.roll(
                summed[at + 2 * pairs : at + 3 * pairs], HALF, 1
            )
            out_ref[pl.ds(step * 2 + parity, pairs, stride=rows), :] = jnp.where(low, even, odd)


def final_kernel(parts_ref, out_ref):
    rows = out_ref.shape[1]
    summed = jnp.sum(parts_ref[...], axis=0)
    for side in range(out_ref.shape[0]):
        out_ref[side] = summed[:, side * HALF : (side + 1) * HALF]


def shards(tiles, coeff, support, row_block, col_block, owner, local_block, metric):
    item_count, width, columns = tiles.shape
    aux_width = metric.shape[1]
    orbitals = support.shape[1]
    aux_count = lax.axis_size("aux")
    pair_count = lax.axis_size("pair")
    groups = orbitals // 2
    pair_steps = (item_count + 1) // 2
    gap = item_count - pair_steps
    vmem = pl.BlockSpec(memory_space=pltpu.VMEM)
    smem = pl.BlockSpec(memory_space=pltpu.SMEM)
    anywhere = pl.BlockSpec(memory_space=pl.ANY)
    small = pltpu.CompilerParams(vmem_limit_bytes=8 * MIB)
    row = lambda array: array.reshape(1, item_count)

    request = pl.pallas_call(
        request_kernel,
        out_shape=jax.ShapeDtypeStruct((aux_count, LANES), jnp.int32),
        in_specs=[vmem] * 3,
        out_specs=vmem,
        name="request",
    )(row(owner), row(local_block), row(col_block))
    asked = lax.all_to_all(
        request.reshape(aux_count, 1, LANES), "aux", split_axis=0, concat_axis=0, tiled=True
    ).reshape(aux_count, LANES)

    late_rows = groups * width
    by_aux = metric.transpose(1, 0, 2)
    depth = -(-aux_width // 8) * 8
    early_count = item_count * 4 // 11
    late_count = item_count - early_count

    def half_scratch(count):
        return [
            pltpu.VMEM((count, width, columns), jnp.bfloat16),
            pltpu.VMEM((2, orbitals, columns), jnp.float32),
            pltpu.VMEM((2, late_rows, LANES), jnp.float32),
            pltpu.SemaphoreType.DMA((2 * count,)),
        ]

    def cost(count):
        return pl.CostEstimate(
            flops=2 * count * orbitals * width * columns,
            bytes_accessed=2 * count * (width * columns + late_rows * LANES),
            transcendentals=0,
        )

    early, padded, picked = pl.pallas_call(
        early_kernel,
        out_shape=[
            jax.ShapeDtypeStruct((early_count, late_rows, LANES), jnp.bfloat16),
            jax.ShapeDtypeStruct((metric.shape[0], depth, LANES), jnp.bfloat16),
            jax.ShapeDtypeStruct((support.shape[0], orbitals, width), jnp.bfloat16),
        ],
        in_specs=[smem, anywhere, vmem, vmem, vmem],
        out_specs=[anywhere, vmem, vmem],
        scratch_shapes=[
            pltpu.VMEM((aux_width * metric.shape[0], LANES), jnp.float32),
            pltpu.VMEM((early_count, late_rows, LANES), jnp.bfloat16),
        ]
        + half_scratch(early_count),
        compiler_params=pltpu.CompilerParams(vmem_limit_bytes=EARLY_LIMIT),
        cost_estimate=cost(early_count),
        name="early",
    )(row_block, tiles, by_aux, coeff, support)

    served = pl.pallas_call(
        serve_kernel,
        out_shape=jax.ShapeDtypeStruct((aux_count, depth, LANES), jnp.bfloat16),
        in_specs=[smem, vmem],
        out_specs=vmem,
        compiler_params=pltpu.CompilerParams(vmem_limit_bytes=SERVE_LIMIT),
        name="serve",
    )(asked, padded)
    metric_tiles = lax.all_to_all(served, "aux", split_axis=0, concat_axis=0, tiled=True)

    picked, _ = lax.optimization_barrier((picked, served))
    late = pl.pallas_call(
        late_kernel,
        out_shape=jax.ShapeDtypeStruct((late_count, late_rows, LANES), jnp.bfloat16),
        in_specs=[smem, anywhere, vmem],
        out_specs=vmem,
        scratch_shapes=half_scratch(late_count),
        compiler_params=pltpu.CompilerParams(vmem_limit_bytes=LATE_LIMIT),
        cost_estimate=cost(late_count),
        name="late",
    )(row_block, tiles, picked)

    cols = asked[:, 32 : 32 + item_count]
    fill = ((0, 0), (0, SLOTS - pair_steps))
    cols_a = jnp.pad(cols[:, :pair_steps], fill, constant_values=-1)
    cols_b = jnp.pad(cols[:, gap:], fill, constant_values=-1)
    cols_b = jnp.where(jnp.arange(SLOTS)[None, :] < pair_steps - gap, -1, cols_b)
    spread = lambda array: jnp.broadcast_to(array[:, None, :], (aux_count, 2, SLOTS)).reshape(1, -1)
    place = jnp.arange(8 * pair_count, dtype=jnp.int32)[:, None]
    block = 2 * (place % pair_count) + place // (2 * pair_count) % 2
    side_b = place // pair_count % 2 == 1
    parity = jnp.arange(aux_count * 2 * SLOTS, dtype=jnp.int32)[None, :] // SLOTS % 2
    hit = jnp.where(side_b, spread(cols_b) == block, spread(cols_a) == block)
    pick = jnp.where(hit & (parity == place // (4 * pair_count)), -1.0, 0.0).astype(jnp.bfloat16)

    blocks = pl.pallas_call(
        term_kernel,
        out_shape=jax.ShapeDtypeStruct((width * SLOTS, LANES), jnp.bfloat16),
        in_specs=[smem, vmem, vmem, vmem],
        out_specs=vmem,
        scratch_shapes=[pltpu.VMEM((width * SLOTS, LANES), jnp.float32)],
        compiler_params=pltpu.CompilerParams(vmem_limit_bytes=TERM_LIMIT),
        name="term",
    )(owner.reshape(item_count), late, early, metric_tiles)
    rows = width // aux_count
    blocks, pick = lax.optimization_barrier((blocks, pick))
    parts = lax.all_to_all(
        blocks.reshape(aux_count, rows * SLOTS, LANES), "aux", split_axis=0, concat_axis=0, tiled=True
    )

    sums = pl.pallas_call(
        combine_kernel,
        out_shape=jax.ShapeDtypeStruct((pair_count * rows, LANES), jnp.float32),
        in_specs=[vmem] * 2,
        out_specs=vmem,
        compiler_params=small,
        name="combine",
    )(parts, pick)
    arrived = lax.all_to_all(
        sums.reshape(pair_count, rows, LANES), "pair", split_axis=0, concat_axis=0, tiled=True
    )
    return pl.pallas_call(
        final_kernel,
        out_shape=jax.ShapeDtypeStruct((2, rows, width), jnp.float32),
        in_specs=[vmem],
        out_specs=vmem,
        compiler_params=small,
        name="final",
    )(arrived)


def solution(mesh):
    return jax.shard_map(
        shards,
        mesh=mesh,
        in_specs=(
            P(("pair", "aux"), None, None),
            P("pair", None),
            P("pair", None),
            P(("pair", "aux")),
            P(("pair", "aux")),
            P(("pair", "aux"), None),
            P(("pair", "aux")),
            P("aux", None, None),
        ),
        out_specs=P("pair", "aux", None),
        check_vma=False,
    )
```

time: 96.4 us -> 81.9 us (0.85)
  blocking collectives: 32.5 us -> 44.2 us
  waiting for transfers between devices: 12.1 us -> 0.59 us
  Pallas kernels: 25.5 us -> 18.8 us
  starting transfers between devices: 17.7 us -> 13.9 us
  local copies, waits for them, and re-layouts: 5.85 us -> 3.45 us
  other arithmetic: 1.93 us -> 0.21 us
    all_to_all x0 -> x1, blocking collectives: none -> 12.9 us  [shards(): lax.all_to_all(blocks.reshape(aux_count, rows * SLOTS, LANES), 'aux', spl...]
    all_to_all x1, waiting for transfers between devices: 6.23 us -> 0.29 us  [shards(): lax.all_to_all(served, 'aux', split_axis=0, concat_axis=0, tiled=True)]
    all_to_all x1 -> x0, waiting for transfers between devices: 5.82 us -> none  [shards(): lax.all_to_all(blocks.reshape(aux_count, rows * SLOTS, LANES), 'aux', spl...]
    pallas_call x3 -> x4, Pallas kernels: 20.6 us -> 16.3 us  [the longest x1 6.03 us: shards(): pl.pallas_call(early_kernel, out_shape=[jax.ShapeDtypeStruct((early_count...]
    all_to_all x1 -> x0, starting transfers between devices: 3.51 us -> none  [shards(): lax.all_to_all(blocks.reshape(aux_count, rows * SLOTS, LANES), 'aux', spl...]
    pallas_call x1, Pallas kernels: 1.85 us -> 0.27 us  [shards(): pl.pallas_call(combine_kernel, out_shape=jax.ShapeDtypeStruct((pair_count...]
    unnamed x9 -> x10, local copies, waits for them, and re-layouts: 4.65 us -> 3.17 us
    all_to_all x1, blocking collectives: 32.5 us -> 31.3 us  [shards(): lax.all_to_all(sums.reshape(pair_count, rows, LANES), 'pair', split_axis=...]
  transfers between devices with their start and end apart: 3 -> 2, of which waited for: 2 -> 2; matrix products, arithmetic and copies ran while one was open for 5% -> 1% of each run, Pallas kernels for 13% -> 14%
where the time goes in v2:
time: 81.9 us; the launch traced here: 81.4 us
  blocking collectives  44.2 us (54%)
  Pallas kernels  18.8 us (23%)
  starting transfers between devices  13.9 us (17%)
  local copies, waits for them, and re-layouts  3.45 us (4%)
    all_to_all x1, blocking collectives, shards(): lax.all_to_all(sums.reshape(pair_count, rows, LANES), 'pair', split_axis=...  31.3 us
    all_to_all x1, blocking collectives, shards(): lax.all_to_all(blocks.reshape(aux_count, rows * SLOTS, LANES), 'aux', spl...  12.9 us
    all_to_all x1, starting transfers between devices, shards(): lax.all_to_all(request.reshape(aux_count, 1, LANES), 'aux', split_axis=0,...  7.58 us
    all_to_all x1, starting transfers between devices, shards(): lax.all_to_all(served, 'aux', split_axis=0, concat_axis=0, tiled=True)  6.36 us
    pallas_call x1, Pallas kernels, shards(): pl.pallas_call(early_kernel, out_shape=[jax.ShapeDtypeStruct((early_count...  6.03 us
    pallas_call x1, Pallas kernels, shards(): pl.pallas_call(late_kernel, out_shape=jax.ShapeDtypeStruct((late_count, l...  5.64 us
    pallas_call x1, Pallas kernels, shards(): pl.pallas_call(term_kernel, out_shape=jax.ShapeDtypeStruct((width * SLOTS...  3.22 us
    unnamed x10, local copies, waits for them, and re-layouts  3.17 us
  transfers between devices with their start and end apart: 2, of which 2 were waited for; matrix products, arithmetic and copies ran while one was open for 1% of the time, Pallas kernels for 14%

profile of v2, /device:TPU:1, one launch (start us, length us, event | category | flops | bytes accessed | tf_op | source)
XLA Modules:
  0.0 81.4 jit_solution(13993850450889358806)
XLA Ops:
  0.0 1.5 %request.1 = s32[16,128]{1,0:T(8,128)} custom-call(s32[1,11]{1,0:T(1,128)} %bitcast.15, s32[1,11]{1,0:T(1,128)} %bitcast.19, s32[1,11]{1,0:T(1,128)} %bitcast.20), custom_call_target="tpu_custom_call" | custom-call | tf_op jit(solution)/shard_map/request/pallas_call | solution.py:229
  1.5 7.6 %all-to-all-start = ((s32[16,1,128]{2,1,0:T(1,128)}), s32[16,1,128]{2,1,0:T(1,128)S(1)}, u32[]{:S(2)}, u32[]{:S(2)}) async-start(s32[16,1,128]{2,1,0:T(1,128)} %bitcast.18), calls=%async_computation | async-start | bytes 16384 | tf_op jit(solution)/shard_map/all_to_all | solution.py:236
  9.2 0.0 copy-start.3
  9.2 6.0 %early.1 = (bf16[4,1536,128]{2,1,0:T(8,128)(2,1)}, bf16[32,56,128]{2,1,0:T(8,128)(2,1)}, bf16[2,48,64]{2,1,0:T(8,128)(2,1)}) custom-call(s32[11]{0:T(128)} %row_ref.3, bf16[11,64,3328]{2,1,0:T(8,128)(2,1)} %tile_ref.3, bf16[52,32,52]{2,1,0:T(8,128)(2,1)} %bitcast.17, bf16[128,256]{1,0:T(8,128)(2,1)} %coeff_ref.1, s32[2,48]{1,0:T(2,128)} %support_ref.1), custom_call_target="tpu_custom_call" | custom-call | flops 81788928 | bytes 3276800 | tf_op jit(solution)/shard_map/early/pallas_call | solution.py:261
  15.2 0.3 all-to-all-done
  15.5 0.1 fusion.9
  15.6 0.0 copy-start.1
  15.6 1.0 %copy-done.1 = bf16[32,56,128]{2,1,0:T(8,128)(2,1)S(1)} copy-done((bf16[32,56,128]{2,1,0:T(8,128)(2,1)S(1)}, bf16[32,56,128]{2,1,0:T(8,128)(2,1)}, u32[]{:S(2)}) %copy-start.1) | copy-done | bytes 458776
  16.6 1.4 %serve.1 = bf16[16,56,128]{2,1,0:T(8,128)(2,1)} custom-call(s32[16,128]{1,0:T(8,128)S(1)} %bitcast.14, bf16[32,56,128]{2,1,0:T(8,128)(2,1)S(1)} %copy-done.1), custom_call_target="tpu_custom_call" | custom-call | tf_op jit(solution)/shard_map/serve/pallas_call | solution.py:280
  18.0 6.4 %all-to-all-start.1 = ((bf16[16,56,128]{2,1,0:T(8,128)(2,1)}), bf16[16,56,128]{2,1,0:T(8,128)(2,1)S(1)}, u32[]{:S(2)}, u32[]{:S(2)}) async-start(bf16[16,56,128]{2,1,0:T(8,128)(2,1)} %serve.1), calls=%async_computation.1 | async-start | bytes 458752 | tf_op jit(solution)/shard_map/all_to_all | solution.py:288
  24.4 0.0 copy-done.3
  24.4 0.0 copy-start.2
  24.4 0.7 copy-done.2
  25.2 0.0 copy-start.4
  25.2 5.6 %late.1.late_ref = bf16[7,1536,128]{2,1,0:T(8,128)(2,1)S(1)} custom-call(s32[11]{0:T(128)S(1)} %copy-done.3, bf16[11,64,3328]{2,1,0:T(8,128)(2,1)} %tile_ref.3, bf16[2,48,64]{2,1,0:T(8,128)(2,1)S(1)} %copy-done.2), custom_call_target="tpu_custom_call" | custom-call | flops 143130624 | bytes 5734400 | tf_op jit(solution)/shard_map/late/pallas_call | solution.py:291
  30.8 0.1 eq.63
  31.0 0.1 eq.59
  31.1 0.2 select_convert_fusion.pick_ref
  31.2 0.3 all-to-all-done.1.metric_ref
  31.5 0.0 copy-done.4
  31.5 0.0 copy-start
  31.5 1.4 %copy-done = bf16[4,1536,128]{2,1,0:T(8,128)(2,1)S(1)} copy-done((bf16[4,1536,128]{2,1,0:T(8,128)(2,1)S(1)}, bf16[4,1536,128]{2,1,0:T(8,128)(2,1)}, u32[]{:S(2)}) %copy-start) | copy-done | bytes 1572888
  32.9 3.2 %term.1 = bf16[512,128]{1,0:T(8,128)(2,1)S(1)} custom-call(s32[11]{0:T(128)S(1)} %bitcast.16, bf16[7,1536,128]{2,1,0:T(8,128)(2,1)S(1)} %late.1.late_ref, bf16[4,1536,128]{2,1,0:T(8,128)(2,1)S(1)} %copy-done, bf16[16,56,128]{2,1,0:T(8,128)(2,1)S(1)} %all-to-all-done.1.metric_ref), custom_call_target="tpu_custom_call" | custom-call | tf_op jit(solution)/shard_map/term/pallas_call | solution.py:315
  36.2 12.9 %all_to_all.20.parts_ref = bf16[16,32,128]{2,1,0:T(8,128)(2,1)S(1)} all-to-all(bf16[16,32,128]{2,1,0:T(8,128)(2,1)S(1)} %bitcast.11), channel_id=1, replica_groups=mesh['pair'=32,'aux'=16] {'aux'}, dimensions={0} | all-to-all | bytes 262144 | tf_op jit(solution)/shard_map/all_to_all | solution.py:326
  49.1 0.3 combine.1
  49.3 31.3 %all_to_all.21.parts_ref = f32[32,4,128]{2,1,0:T(4,128)S(1)} all-to-all(f32[32,4,128]{2,1,0:T(4,128)S(1)} %bitcast.12), channel_id=1, replica_groups=mesh['pair'=32,'aux'=16] {'pair'}, dimensions={0} | all-to-all | bytes 131072 | tf_op jit(solution)/shard_map/all_to_all | solution.py:338
  80.7 0.7 final.1
  (8 shorter events, 0.1 us)
Async XLA Ops:
  1.5 14.0 %all-to-all-start = ((s32[16,1,128]{2,1,0:T(1,128)}), s32[16,1,128]{2,1,0:T(1,128)S(1)}, u32[]{:S(2)}, u32[]{:S(2)}) async-start(s32[16,1,128]{2,1,0:T(1,128)} %bitcast.18), calls=%async_computation | async-start | bytes 16384 | tf_op jit(solution)/shard_map/all_to_all | solution.py:236
  9.2 15.2 %copy-start.3 = (s32[11]{0:T(128)S(1)}, s32[11]{0:T(128)}, u32[]{:S(2)}) copy-start(s32[11]{0:T(128)} %row_ref.3) | copy-start | bytes 136
  15.6 1.0 %copy-start.1 = (bf16[32,56,128]{2,1,0:T(8,128)(2,1)S(1)}, bf16[32,56,128]{2,1,0:T(8,128)(2,1)}, u32[]{:S(2)}) copy-start(bf16[32,56,128]{2,1,0:T(8,128)(2,1)} %get-tuple-element.12.metric_ref) | copy-start | bytes 1376260
  18.0 13.5 %all-to-all-start.1 = ((bf16[16,56,128]{2,1,0:T(8,128)(2,1)}), bf16[16,56,128]{2,1,0:T(8,128)(2,1)S(1)}, u32[]{:S(2)}, u32[]{:S(2)}) async-start(bf16[16,56,128]{2,1,0:T(8,128)(2,1)} %serve.1), calls=%async_computation.1 | async-start | bytes 458752 | tf_op jit(solution)/shard_map/all_to_all | solution.py:288
  24.4 0.7 copy-start.2
  25.2 6.4 %copy-start.4 = (s32[11,1]{0,1:T(1,128)S(1)}, s32[11,1]{0,1:T(1,128)}, u32[]{:S(2)}) copy-start(s32[11,1]{0,1:T(1,128)} %param.13) | copy-start | bytes 136
  31.5 1.4 %copy-start = (bf16[4,1536,128]{2,1,0:T(8,128)(2,1)S(1)}, bf16[4,1536,128]{2,1,0:T(8,128)(2,1)}, u32[]{:S(2)}) copy-start(bf16[4,1536,128]{2,1,0:T(8,128)(2,1)} %get-tuple-element.14.early_ref) | copy-start | bytes 4718596

commit v3 on v2

--- a/solution.py
+++ b/solution.py
@@ -8,8 +8,8 @@
 LANES = 128
 HALF = 64
 MIB = 1 << 20
-EARLY_LIMIT = 61_000_000
-SERVE_LIMIT = 55_700_000
+EARLY_LIMIT = 55_200_000
+SERVE_LIMIT = 8 * MIB
 LATE_LIMIT = 51_000_000
 TERM_LIMIT = 51_000_000
 SLOTS = 8
@@ -240,7 +240,7 @@
     late_rows = groups * width
     by_aux = metric.transpose(1, 0, 2)
     depth = -(-aux_width // 8) * 8
-    early_count = item_count * 4 // 11
+    early_count = item_count * 3 // 11
     late_count = item_count - early_count
 
     def half_scratch(count):

time: 81.9 us -> 81.9 us (level)
  local copies, waits for them, and re-layouts: 3.45 us -> 4.74 us
  Pallas kernels: 18.8 us -> 17.6 us
    pallas_call x1, Pallas kernels: 6.03 us -> 4.14 us  [shards(): pl.pallas_call(early_kernel, out_shape=[jax.ShapeDtypeStruct((early_count...]
    unnamed x10 -> x14, local copies, waits for them, and re-layouts: 3.17 us -> 4.46 us
  transfers between devices with their start and end apart: 2 -> 2, of which waited for: 2 -> 1; matrix products, arithmetic and copies ran while one was open for 1% -> 1% of each run, Pallas kernels for 14% -> 13%
where the time goes in v3:
time: 81.9 us; the launch traced here: 81.4 us
  blocking collectives  44.1 us (54%)
  Pallas kernels  17.6 us (21%)
  starting transfers between devices  14.2 us (17%)
  local copies, waits for them, and re-layouts  4.74 us (6%)
    all_to_all x1, blocking collectives, shards(): lax.all_to_all(sums.reshape(pair_count, rows, LANES), 'pair', split_axis=...  31.3 us
    all_to_all x1, blocking collectives, shards(): lax.all_to_all(blocks.reshape(aux_count, rows * SLOTS, LANES), 'aux', spl...  12.8 us
    all_to_all x1, starting transfers between devices, shards(): lax.all_to_all(request.reshape(aux_count, 1, LANES), 'aux', split_axis=0,...  7.58 us
    all_to_all x1, starting transfers between devices, shards(): lax.all_to_all(served, 'aux', split_axis=0, concat_axis=0, tiled=True)  6.65 us
    pallas_call x1, Pallas kernels, shards(): pl.pallas_call(late_kernel, out_shape=jax.ShapeDtypeStruct((late_count, l...  6.25 us
    unnamed x14, local copies, waits for them, and re-layouts  4.46 us
    pallas_call x1, Pallas kernels, shards(): pl.pallas_call(early_kernel, out_shape=[jax.ShapeDtypeStruct((early_count...  4.14 us
    pallas_call x1, Pallas kernels, shards(): pl.pallas_call(term_kernel, out_shape=jax.ShapeDtypeStruct((width * SLOTS...  3.22 us
  transfers between devices with their start and end apart: 2, of which 1 were waited for; matrix products, arithmetic and copies ran while one was open for 1% of the time, Pallas kernels for 13%

profile of v3, /device:TPU:1, one launch (start us, length us, event | category | flops | bytes accessed | tf_op | source)
XLA Modules:
  0.0 81.4 jit_solution(7409777093521317437)
XLA Ops:
  0.0 1.5 %request.1 = s32[16,128]{1,0:T(8,128)} custom-call(s32[1,11]{1,0:T(1,128)} %bitcast.16, s32[1,11]{1,0:T(1,128)} %bitcast.19, s32[1,11]{1,0:T(1,128)} %bitcast.20), custom_call_target="tpu_custom_call" | custom-call | tf_op jit(solution)/shard_map/request/pallas_call | solution.py:229
  1.5 7.6 %all-to-all-start = ((s32[16,1,128]{2,1,0:T(1,128)}), s32[16,1,128]{2,1,0:T(1,128)S(1)}, u32[]{:S(2)}, u32[]{:S(2)}) async-start(s32[16,1,128]{2,1,0:T(1,128)} %bitcast.18), calls=%async_computation | async-start | bytes 16384 | tf_op jit(solution)/shard_map/all_to_all | solution.py:236
  9.2 0.0 copy-start.1
  9.2 1.0 %copy-done.1 = bf16[32,52,52]{2,0,1:T(8,128)(2,1)S(1)} copy-done((bf16[32,52,52]{2,0,1:T(8,128)(2,1)S(1)}, bf16[32,52,52]{2,0,1:T(8,128)(2,1)}, u32[]{:S(2)}) %copy-start.1) | copy-done | bytes 173080
  10.2 0.0 copy-start.2
  10.2 0.8 %copy-done.2 = bf16[128,256]{1,0:T(8,128)(2,1)S(1)} copy-done((bf16[128,256]{1,0:T(8,128)(2,1)S(1)}, bf16[128,256]{1,0:T(8,128)(2,1)}, u32[]{:S(2)}) %copy-start.2) | copy-done | bytes 65560
  11.0 0.0 copy-start.3
  11.0 0.7 copy-done.3
  11.7 0.0 copy-start.6
  11.7 0.7 copy-done.6
  12.4 0.0 copy-start.4
  12.4 4.1 %early.1 = (bf16[3,1536,128]{2,1,0:T(8,128)(2,1)}, bf16[32,56,128]{2,1,0:T(8,128)(2,1)S(1)}, bf16[2,48,64]{2,1,0:T(8,128)(2,1)S(1)}) custom-call(s32[11]{0:T(128)S(1)} %copy-done.3, bf16[11,64,3328]{2,1,0:T(8,128)(2,1)} %tile_ref.3, bf16[52,32,52]{2,1,0:T(8,128)(2,1)S(1)} %bitcast.12, bf16[128,256]{1,0:T(8,128)(2,1)S(1)} %copy-done.2, s32[2,48]{1,0:T(2,128)S(1)} %copy-done.6), custom_call_target="tpu_custom_call" | custom-call | flops 61341696 | bytes 2457600 | tf_op jit(solution)/shard_map/early/pallas_call | solution.py:261
  16.5 0.0 all-to-all-done
  16.5 0.1 fusion.9
  16.6 1.4 %serve.1 = bf16[16,56,128]{2,1,0:T(8,128)(2,1)} custom-call(s32[16,128]{1,0:T(8,128)S(1)} %bitcast.15, bf16[32,56,128]{2,1,0:T(8,128)(2,1)S(1)} %get-tuple-element.12.metric_ref), custom_call_target="tpu_custom_call" | custom-call | tf_op jit(solution)/shard_map/serve/pallas_call | solution.py:280
  18.0 6.6 %all-to-all-start.1 = ((bf16[16,56,128]{2,1,0:T(8,128)(2,1)}), bf16[16,56,128]{2,1,0:T(8,128)(2,1)S(1)}, u32[]{:S(2)}, u32[]{:S(2)}) async-start(bf16[16,56,128]{2,1,0:T(8,128)(2,1)} %serve.1), calls=%async_computation.1 | async-start | bytes 458752 | tf_op jit(solution)/shard_map/all_to_all | solution.py:288
  24.7 0.0 copy-done.4
  24.7 0.0 copy-start.5
  24.7 6.3 %late.1.late_ref = bf16[8,1536,128]{2,1,0:T(8,128)(2,1)S(1)} custom-call(s32[11]{0:T(128)S(1)} %copy-done.4, bf16[11,64,3328]{2,1,0:T(8,128)(2,1)} %tile_ref.3, bf16[2,48,64]{2,1,0:T(8,128)(2,1)S(1)} %get-tuple-element.13.picked_ref), custom_call_target="tpu_custom_call" | custom-call | flops 163577856 | bytes 6553600 | tf_op jit(solution)/shard_map/late/pallas_call | solution.py:291
  31.0 0.1 eq.63
  31.1 0.1 eq.59
  31.2 0.2 select_convert_fusion.pick_ref
  31.4 0.4 all-to-all-done.1.metric_ref
  31.8 0.0 copy-done.5
  31.8 0.0 copy-start
  31.8 1.3 %copy-done = bf16[3,1536,128]{2,1,0:T(8,128)(2,1)S(1)} copy-done((bf16[3,1536,128]{2,1,0:T(8,128)(2,1)S(1)}, bf16[3,1536,128]{2,1,0:T(8,128)(2,1)}, u32[]{:S(2)}) %copy-start) | copy-done | bytes 1179672
  33.1 3.2 %term.1 = bf16[512,128]{1,0:T(8,128)(2,1)S(1)} custom-call(s32[11]{0:T(128)S(1)} %bitcast.17, bf16[8,1536,128]{2,1,0:T(8,128)(2,1)S(1)} %late.1.late_ref, bf16[3,1536,128]{2,1,0:T(8,128)(2,1)S(1)} %copy-done, bf16[16,56,128]{2,1,0:T(8,128)(2,1)S(1)} %all-to-all-done.1.metric_ref), custom_call_target="tpu_custom_call" | custom-call | tf_op jit(solution)/shard_map/term/pallas_call | solution.py:315
  36.3 12.8 %all_to_all.20.parts_ref = bf16[16,32,128]{2,1,0:T(8,128)(2,1)S(1)} all-to-all(bf16[16,32,128]{2,1,0:T(8,128)(2,1)S(1)} %bitcast.11), channel_id=1, replica_groups=mesh['pair'=32,'aux'=16] {'aux'}, dimensions={0} | all-to-all | bytes 262144 | tf_op jit(solution)/shard_map/all_to_all | solution.py:326
  49.1 0.3 combine.1
  49.3 31.3 %all_to_all.21.parts_ref = f32[32,4,128]{2,1,0:T(4,128)S(1)} all-to-all(f32[32,4,128]{2,1,0:T(4,128)S(1)} %bitcast.13), channel_id=1, replica_groups=mesh['pair'=32,'aux'=16] {'pair'}, dimensions={0} | all-to-all | bytes 131072 | tf_op jit(solution)/shard_map/all_to_all | solution.py:338
  80.7 0.7 final.1
  (8 shorter events, 0.1 us)
Async XLA Ops:
  1.5 15.0 %all-to-all-start = ((s32[16,1,128]{2,1,0:T(1,128)}), s32[16,1,128]{2,1,0:T(1,128)S(1)}, u32[]{:S(2)}, u32[]{:S(2)}) async-start(s32[16,1,128]{2,1,0:T(1,128)} %bitcast.18), calls=%async_computation | async-start | bytes 16384 | tf_op jit(solution)/shard_map/all_to_all | solution.py:236
  9.2 1.0 %copy-start.1 = (bf16[32,52,52]{2,0,1:T(8,128)(2,1)S(1)}, bf16[32,52,52]{2,0,1:T(8,128)(2,1)}, u32[]{:S(2)}) copy-start(bf16[32,52,52]{2,0,1:T(8,128)(2,1)} %param.15) | copy-start | bytes 519172
  10.2 0.8 %copy-start.2 = (bf16[128,256]{1,0:T(8,128)(2,1)S(1)}, bf16[128,256]{1,0:T(8,128)(2,1)}, u32[]{:S(2)}) copy-start(bf16[128,256]{1,0:T(8,128)(2,1)} %coeff_ref.1) | copy-start | bytes 196612
  11.0 0.7 copy-start.3
  11.7 0.7 copy-start.6
  12.4 12.3 %copy-start.4 = (s32[11]{0:T(128)S(1)}, s32[11]{0:T(128)}, u32[]{:S(2)}) copy-start(s32[11]{0:T(128)} %row_ref.3) | copy-start | bytes 136
  18.0 13.8 %all-to-all-start.1 = ((bf16[16,56,128]{2,1,0:T(8,128)(2,1)}), bf16[16,56,128]{2,1,0:T(8,128)(2,1)S(1)}, u32[]{:S(2)}, u32[]{:S(2)}) async-start(bf16[16,56,128]{2,1,0:T(8,128)(2,1)} %serve.1), calls=%async_computation.1 | async-start | bytes 458752 | tf_op jit(solution)/shard_map/all_to_all | solution.py:288
  24.7 7.1 %copy-start.5 = (s32[11,1]{0,1:T(1,128)S(1)}, s32[11,1]{0,1:T(1,128)}, u32[]{:S(2)}) copy-start(s32[11,1]{0,1:T(1,128)} %param.13) | copy-start | bytes 136
  31.8 1.3 %copy-start = (bf16[3,1536,128]{2,1,0:T(8,128)(2,1)S(1)}, bf16[3,1536,128]{2,1,0:T(8,128)(2,1)}, u32[]{:S(2)}) copy-start(bf16[3,1536,128]{2,1,0:T(8,128)(2,1)} %get-tuple-element.14.early_ref) | copy-start | bytes 3538948

commit v4 on v3

--- a/solution.py
+++ b/solution.py
@@ -8,6 +8,7 @@
 LANES = 128
 HALF = 64
 MIB = 1 << 20
+EARLY_ROOM = 40
 EARLY_LIMIT = 55_200_000
 SERVE_LIMIT = 8 * MIB
 LATE_LIMIT = 51_000_000
@@ -133,9 +134,10 @@
         )
 
 
-def term_kernel(owner_ref, late_ref, early_ref, metric_ref, out_ref, total):
+def term_kernel(owner_ref, late_ref, early_ref, metric_ref, out_ref, buffer_ref, total, sems):
     late_count, rows, _ = late_ref.shape
-    item_count = late_count + early_ref.shape[0]
+    item_count = late_count + buffer_ref.shape[0]
+    copies = fetch(early_ref, 0, buffer_ref, sems)
     width = out_ref.shape[0] // SLOTS
     depth = metric_ref.shape[1]
     steps = (item_count + 1) // 2
@@ -162,7 +164,11 @@
         )
 
     def term(item):
-        halves = late_ref[item] if item < late_count else early_ref[item - late_count]
+        if item < late_count:
+            halves = late_ref[item]
+        else:
+            copies[item - late_count].wait()
+            halves = buffer_ref[item - late_count]
         fitted = jnp.dot(halves, placed(item), preferred_element_type=jnp.float32)
         return lax.dot_general(
             spread(halves),
@@ -261,7 +267,7 @@
     early, padded, picked = pl.pallas_call(
         early_kernel,
         out_shape=[
-            jax.ShapeDtypeStruct((early_count, late_rows, LANES), jnp.bfloat16),
+            jax.ShapeDtypeStruct((EARLY_ROOM, late_rows, LANES), jnp.bfloat16),
             jax.ShapeDtypeStruct((metric.shape[0], depth, LANES), jnp.bfloat16),
             jax.ShapeDtypeStruct((support.shape[0], orbitals, width), jnp.bfloat16),
         ],
@@ -315,9 +321,13 @@
     blocks = pl.pallas_call(
         term_kernel,
         out_shape=jax.ShapeDtypeStruct((width * SLOTS, LANES), jnp.bfloat16),
-        in_specs=[smem, vmem, vmem, vmem],
-        out_specs=vmem,
-        scratch_shapes=[pltpu.VMEM((width * SLOTS, LANES), jnp.float32)],
+        in_specs=[smem, vmem, anywhere, vmem],
+        out_specs=vmem,
+        scratch_shapes=[
+            pltpu.VMEM((early_count, late_rows, LANES), jnp.bfloat16),
+            pltpu.VMEM((width * SLOTS, LANES), jnp.float32),
+            pltpu.SemaphoreType.DMA((early_count,)),
+        ],
         compiler_params=pltpu.CompilerParams(vmem_limit_bytes=TERM_LIMIT),
         name="term",
     )(owner.reshape(item_count), late, early, metric_tiles)

time: 81.9 us -> 82.6 us (level)
  Pallas kernels: 17.6 us -> 19.6 us
  local copies, waits for them, and re-layouts: 4.74 us -> 3.47 us
    pallas_call x1, Pallas kernels: 3.22 us -> 5.21 us  [shards(): pl.pallas_call(term_kernel, out_shape=jax.ShapeDtypeStruct((width * SLOTS...]
    unnamed x14 -> x12, local copies, waits for them, and re-layouts: 4.46 us -> 3.18 us
where the time goes in v4:
time: 82.6 us; the launch traced here: 82.1 us
  blocking collectives  44.1 us (53%)
  Pallas kernels  19.6 us (24%)
  starting transfers between devices  14.2 us (17%)
  local copies, waits for them, and re-layouts  3.47 us (4%)
    all_to_all x1, blocking collectives, shards(): lax.all_to_all(sums.reshape(pair_count, rows, LANES), 'pair', split_axis=...  31.4 us
    all_to_all x1, blocking collectives, shards(): lax.all_to_all(blocks.reshape(aux_count, rows * SLOTS, LANES), 'aux', spl...  12.7 us
    all_to_all x1, starting transfers between devices, shards(): lax.all_to_all(request.reshape(aux_count, 1, LANES), 'aux', split_axis=0,...  7.58 us
    all_to_all x1, starting transfers between devices, shards(): lax.all_to_all(served, 'aux', split_axis=0, concat_axis=0, tiled=True)  6.66 us
    pallas_call x1, Pallas kernels, shards(): pl.pallas_call(late_kernel, out_shape=jax.ShapeDtypeStruct((late_count, l...  6.27 us
    pallas_call x1, Pallas kernels, shards(): pl.pallas_call(term_kernel, out_shape=jax.ShapeDtypeStruct((width * SLOTS...  5.21 us
    pallas_call x1, Pallas kernels, shards(): pl.pallas_call(early_kernel, out_shape=[jax.ShapeDtypeStruct((EARLY_ROOM,...  4.13 us
    unnamed x12, local copies, waits for them, and re-layouts  3.18 us
  transfers between devices with their start and end apart: 2, of which 1 were waited for; matrix products, arithmetic and copies ran while one was open for 1% of the time, Pallas kernels for 13%

profile of v4, /device:TPU:1, one launch (start us, length us, event | category | flops | bytes accessed | tf_op | source)
XLA Modules:
  0.0 82.1 jit_solution(10621049299219211023)
XLA Ops:
  0.0 0.0 copy-start.3
  0.0 1.5 %request.1 = s32[16,128]{1,0:T(8,128)} custom-call(s32[1,11]{1,0:T(1,128)} %bitcast.16, s32[1,11]{1,0:T(1,128)} %bitcast.19, s32[1,11]{1,0:T(1,128)} %bitcast.20), custom_call_target="tpu_custom_call" | custom-call | tf_op jit(solution)/shard_map/request/pallas_call | solution.py:235
  1.5 7.6 %all-to-all-start = ((s32[16,1,128]{2,1,0:T(1,128)}), s32[16,1,128]{2,1,0:T(1,128)S(1)}, u32[]{:S(2)}, u32[]{:S(2)}) async-start(s32[16,1,128]{2,1,0:T(1,128)} %bitcast.18), calls=%async_computation | async-start | bytes 16384 | tf_op jit(solution)/shard_map/all_to_all | solution.py:242
  9.2 0.0 copy-start
  9.2 1.0 %copy-done = bf16[32,52,52]{2,0,1:T(8,128)(2,1)S(1)} copy-done((bf16[32,52,52]{2,0,1:T(8,128)(2,1)S(1)}, bf16[32,52,52]{2,0,1:T(8,128)(2,1)}, u32[]{:S(2)}) %copy-start) | copy-done | bytes 173080
  10.2 0.0 copy-start.1
  10.2 0.8 %copy-done.1 = bf16[128,256]{1,0:T(8,128)(2,1)S(1)} copy-done((bf16[128,256]{1,0:T(8,128)(2,1)S(1)}, bf16[128,256]{1,0:T(8,128)(2,1)}, u32[]{:S(2)}) %copy-start.1) | copy-done | bytes 65560
  11.0 0.0 copy-start.2
  11.0 0.7 copy-done.2
  11.7 0.0 copy-start.5
  11.7 0.7 copy-done.5
  12.4 4.1 %early.1 = (bf16[40,1536,128]{2,1,0:T(8,128)(2,1)}, bf16[32,56,128]{2,1,0:T(8,128)(2,1)S(1)}, bf16[2,48,64]{2,1,0:T(8,128)(2,1)S(1)}) custom-call(s32[11]{0:T(128)S(1)} %copy-done.2, bf16[11,64,3328]{2,1,0:T(8,128)(2,1)} %tile_ref.3, bf16[52,32,52]{2,1,0:T(8,128)(2,1)S(1)} %bitcast.12, bf16[128,256]{1,0:T(8,128)(2,1)S(1)} %copy-done.1, s32[2,48]{1,0:T(2,128)S(1)} %copy-done.5), custom_call_target="tpu_custom_call" | custom-call | flops 61341696 | bytes 2457600 | tf_op jit(solution)/shard_map/early/pallas_call | solution.py:267
  16.5 0.0 copy-start.4
  16.5 0.0 all-to-all-done
  16.5 0.1 fusion.9
  16.6 1.4 %serve.1 = bf16[16,56,128]{2,1,0:T(8,128)(2,1)} custom-call(s32[16,128]{1,0:T(8,128)S(1)} %bitcast.15, bf16[32,56,128]{2,1,0:T(8,128)(2,1)S(1)} %get-tuple-element.12.metric_ref), custom_call_target="tpu_custom_call" | custom-call | tf_op jit(solution)/shard_map/serve/pallas_call | solution.py:286
  18.1 6.7 %all-to-all-start.1 = ((bf16[16,56,128]{2,1,0:T(8,128)(2,1)}), bf16[16,56,128]{2,1,0:T(8,128)(2,1)S(1)}, u32[]{:S(2)}, u32[]{:S(2)}) async-start(bf16[16,56,128]{2,1,0:T(8,128)(2,1)} %serve.1), calls=%async_computation.1 | async-start | bytes 458752 | tf_op jit(solution)/shard_map/all_to_all | solution.py:294
  24.7 0.0 copy-done.3
  24.7 6.3 %late.1.late_ref = bf16[8,1536,128]{2,1,0:T(8,128)(2,1)S(1)} custom-call(s32[11]{0:T(128)S(1)} %copy-done.3, bf16[11,64,3328]{2,1,0:T(8,128)(2,1)} %tile_ref.3, bf16[2,48,64]{2,1,0:T(8,128)(2,1)S(1)} %get-tuple-element.13.picked_ref), custom_call_target="tpu_custom_call" | custom-call | flops 163577856 | bytes 6553600 | tf_op jit(solution)/shard_map/late/pallas_call | solution.py:297
  31.0 0.1 eq.63
  31.2 0.1 eq.59
  31.3 0.2 select_convert_fusion.pick_ref
  31.4 0.4 all-to-all-done.1.metric_ref
  31.8 0.0 copy-done.4
  31.8 5.2 %term.1 = bf16[512,128]{1,0:T(8,128)(2,1)S(1)} custom-call(s32[11]{0:T(128)S(1)} %bitcast.17, bf16[8,1536,128]{2,1,0:T(8,128)(2,1)S(1)} %late.1.late_ref, bf16[40,1536,128]{2,1,0:T(8,128)(2,1)} %get-tuple-element.14.early_ref, bf16[16,56,128]{2,1,0:T(8,128)(2,1)S(1)} %all-to-all-done.1.metric_ref), custom_call_target="tpu_custom_call" | custom-call | tf_op jit(solution)/shard_map/term/pallas_call | solution.py:321
  37.1 12.7 %all_to_all.20.parts_ref = bf16[16,32,128]{2,1,0:T(8,128)(2,1)S(1)} all-to-all(bf16[16,32,128]{2,1,0:T(8,128)(2,1)S(1)} %bitcast.11), channel_id=1, replica_groups=mesh['pair'=32,'aux'=16] {'aux'}, dimensions={0} | all-to-all | bytes 262144 | tf_op jit(solution)/shard_map/all_to_all | solution.py:336
  49.8 0.3 combine.1
  50.1 31.4 %all_to_all.21.parts_ref = f32[32,4,128]{2,1,0:T(4,128)S(1)} all-to-all(f32[32,4,128]{2,1,0:T(4,128)S(1)} %bitcast.13), channel_id=1, replica_groups=mesh['pair'=32,'aux'=16] {'pair'}, dimensions={0} | all-to-all | bytes 131072 | tf_op jit(solution)/shard_map/all_to_all | solution.py:348
  81.4 0.7 final.1
  (8 shorter events, 0.1 us)
Async XLA Ops:
  0.0 24.7 %copy-start.3 = (s32[11]{0:T(128)S(1)}, s32[11]{0:T(128)}, u32[]{:S(2)}) copy-start(s32[11]{0:T(128)} %row_ref.3) | copy-start | bytes 136
  1.5 15.0 %all-to-all-start = ((s32[16,1,128]{2,1,0:T(1,128)}), s32[16,1,128]{2,1,0:T(1,128)S(1)}, u32[]{:S(2)}, u32[]{:S(2)}) async-start(s32[16,1,128]{2,1,0:T(1,128)} %bitcast.18), calls=%async_computation | async-start | bytes 16384 | tf_op jit(solution)/shard_map/all_to_all | solution.py:242
  9.2 1.0 %copy-start = (bf16[32,52,52]{2,0,1:T(8,128)(2,1)S(1)}, bf16[32,52,52]{2,0,1:T(8,128)(2,1)}, u32[]{:S(2)}) copy-start(bf16[32,52,52]{2,0,1:T(8,128)(2,1)} %param.15) | copy-start | bytes 519172
  10.2 0.8 %copy-start.1 = (bf16[128,256]{1,0:T(8,128)(2,1)S(1)}, bf16[128,256]{1,0:T(8,128)(2,1)}, u32[]{:S(2)}) copy-start(bf16[128,256]{1,0:T(8,128)(2,1)} %coeff_ref.1) | copy-start | bytes 196612
  11.0 0.7 copy-start.2
  11.7 0.7 copy-start.5
  16.5 15.3 %copy-start.4 = (s32[11,1]{0,1:T(1,128)S(1)}, s32[11,1]{0,1:T(1,128)}, u32[]{:S(2)}) copy-start(s32[11,1]{0,1:T(1,128)} %param.13) | copy-start | bytes 136
  18.1 13.8 %all-to-all-start.1 = ((bf16[16,56,128]{2,1,0:T(8,128)(2,1)}), bf16[16,56,128]{2,1,0:T(8,128)(2,1)S(1)}, u32[]{:S(2)}, u32[]{:S(2)}) async-start(bf16[16,56,128]{2,1,0:T(8,128)(2,1)} %serve.1), calls=%async_computation.1 | async-start | bytes 458752 | tf_op jit(solution)/shard_map/all_to_all | solution.py:294

commit v5 on v3

--- a/solution.py
+++ b/solution.py
@@ -1,3 +1,4 @@
+import functools
 import jax
 import jax.numpy as jnp
 from jax import lax
@@ -133,13 +134,12 @@
         )
 
 
-def term_kernel(owner_ref, late_ref, early_ref, metric_ref, out_ref, total):
-    late_count, rows, _ = late_ref.shape
-    item_count = late_count + early_ref.shape[0]
-    width = out_ref.shape[0] // SLOTS
+def term_kernel(first, first_slot, owner_ref, halves_ref, metric_ref, *refs):
+    *before, out_ref, total = refs
+    item_count, rows, _ = halves_ref.shape
+    width = total.shape[0] // SLOTS
     depth = metric_ref.shape[1]
     steps = (item_count + 1) // 2
-    gap = item_count - steps
     groups = rows // width
     lane = lax.broadcasted_iota(jnp.int32, (depth, LANES), 1)
     rest = jnp.zeros((HALF - depth, LANES), jnp.float32)
@@ -162,8 +162,10 @@
         )
 
     def term(item):
-        halves = late_ref[item] if item < late_count else early_ref[item - late_count]
-        fitted = jnp.dot(halves, placed(item), preferred_element_type=jnp.float32)
+        if item >= item_count:
+            return jnp.zeros((width, HALF), jnp.float32)
+        halves = halves_ref[item]
+        fitted = jnp.dot(halves, placed(first + item), preferred_element_type=jnp.float32)
         return lax.dot_general(
             spread(halves),
             spread(fitted.astype(jnp.bfloat16)),
@@ -171,16 +173,12 @@
             preferred_element_type=jnp.float32,
         )
 
-    total[...] = jnp.zeros_like(total)
-    terms = []
-    for item in range(item_count):
-        terms.append(term(item))
-        if item >= gap and item - gap < steps:
-            at = item - gap
-            total[pl.ds(at, width, stride=SLOTS), :] = jnp.concatenate(
-                [terms[at], terms[item]], axis=1
-            )
-    out_ref[...] = total[...].astype(jnp.bfloat16)
+    total[...] = before[0][...] if before else jnp.zeros_like(total)
+    for step in range(steps):
+        total[pl.ds(first_slot + step, width, stride=SLOTS), :] = jnp.concatenate(
+            [term(step), term(step + steps)], axis=1
+        )
+    out_ref[...] = total[...].astype(out_ref.dtype)
 
 
 def combine_kernel(parts_ref, pick_ref, out_ref):
@@ -218,8 +216,6 @@
     aux_count = lax.axis_size("aux")
     pair_count = lax.axis_size("pair")
     groups = orbitals // 2
-    pair_steps = (item_count + 1) // 2
-    gap = item_count - pair_steps
     vmem = pl.BlockSpec(memory_space=pltpu.VMEM)
     smem = pl.BlockSpec(memory_space=pltpu.SMEM)
     anywhere = pl.BlockSpec(memory_space=pl.ANY)
@@ -300,10 +296,22 @@
     )(row_block, tiles, picked)
 
     cols = asked[:, 32 : 32 + item_count]
-    fill = ((0, 0), (0, SLOTS - pair_steps))
-    cols_a = jnp.pad(cols[:, :pair_steps], fill, constant_values=-1)
-    cols_b = jnp.pad(cols[:, gap:], fill, constant_values=-1)
-    cols_b = jnp.where(jnp.arange(SLOTS)[None, :] < pair_steps - gap, -1, cols_b)
+    late_steps, early_steps = (late_count + 1) // 2, (early_count + 1) // 2
+
+    def columns_of(*parts):
+        taken = []
+        for start, stop, size in parts:
+            fill = ((0, 0), (0, size - (stop - start)))
+            taken.append(jnp.pad(cols[:, start:stop], fill, constant_values=-1))
+        return jnp.concatenate(taken, axis=1)
+
+    spare = SLOTS - late_steps
+    cols_a = columns_of(
+        (0, late_steps, late_steps), (late_count, late_count + early_steps, spare)
+    )
+    cols_b = columns_of(
+        (late_steps, late_count, late_steps), (late_count + early_steps, item_count, spare)
+    )
     spread = lambda array: jnp.broadcast_to(array[:, None, :], (aux_count, 2, SLOTS)).reshape(1, -1)
     place = jnp.arange(8 * pair_count, dtype=jnp.int32)[:, None]
     block = 2 * (place % pair_count) + place // (2 * pair_count) % 2
@@ -312,15 +320,24 @@
     hit = jnp.where(side_b, spread(cols_b) == block, spread(cols_a) == block)
     pick = jnp.where(hit & (parity == place // (4 * pair_count)), -1.0, 0.0).astype(jnp.bfloat16)
 
-    blocks = pl.pallas_call(
-        term_kernel,
-        out_shape=jax.ShapeDtypeStruct((width * SLOTS, LANES), jnp.bfloat16),
-        in_specs=[smem, vmem, vmem, vmem],
-        out_specs=vmem,
-        scratch_shapes=[pltpu.VMEM((width * SLOTS, LANES), jnp.float32)],
-        compiler_params=pltpu.CompilerParams(vmem_limit_bytes=TERM_LIMIT),
-        name="term",
-    )(owner.reshape(item_count), late, early, metric_tiles)
+    def terms(first, first_slot, halves, before, dtype, name):
+        return pl.pallas_call(
+            functools.partial(term_kernel, first, first_slot),
+            out_shape=jax.ShapeDtypeStruct((width * SLOTS, LANES), dtype),
+            in_specs=[smem] + [vmem] * (2 + len(before)),
+            out_specs=vmem,
+            scratch_shapes=[pltpu.VMEM((width * SLOTS, LANES), jnp.float32)],
+            compiler_params=pltpu.CompilerParams(vmem_limit_bytes=TERM_LIMIT),
+            cost_estimate=pl.CostEstimate(
+                flops=2 * halves.shape[0] * late_rows * LANES * (LANES + width),
+                bytes_accessed=2 * halves.size,
+                transcendentals=0,
+            ),
+            name=name,
+        )(owner.reshape(item_count), halves, metric_tiles, *before)
+
+    blocks = terms(0, 0, late, (), jnp.float32, "late_term")
+    blocks = terms(late_count, late_steps, early, (blocks,), jnp.bfloat16, "early_term")
     rows = width // aux_count
     blocks, pick = lax.optimization_barrier((blocks, pick))
     parts = lax.all_to_all(

time: 81.9 us -> 81.7 us (level)
  local copies, waits for them, and re-layouts: 4.74 us -> 3.61 us
  Pallas kernels: 17.6 us -> 18.5 us
    unnamed x14, local copies, waits for them, and re-layouts: 4.46 us -> 3.19 us
    pallas_call x1 -> x2, Pallas kernels: 3.22 us -> 4.14 us  [terms(): pl.pallas_call(functools.partial(term_kernel, first, first_slot), out_sha...]
where the time goes in v5:
time: 81.7 us; the launch traced here: 81.2 us
  blocking collectives  44.2 us (54%)
  Pallas kernels  18.5 us (23%)
  starting transfers between devices  14.2 us (17%)
  local copies, waits for them, and re-layouts  3.61 us (4%)
    all_to_all x1, blocking collectives, shards(): lax.all_to_all(sums.reshape(pair_count, rows, LANES), 'pair', split_axis=...  31.3 us
    all_to_all x1, blocking collectives, shards(): lax.all_to_all(blocks.reshape(aux_count, rows * SLOTS, LANES), 'aux', spl...  12.8 us
    all_to_all x1, starting transfers between devices, shards(): lax.all_to_all(request.reshape(aux_count, 1, LANES), 'aux', split_axis=0,...  7.58 us
    all_to_all x1, starting transfers between devices, shards(): lax.all_to_all(served, 'aux', split_axis=0, concat_axis=0, tiled=True)  6.65 us
    pallas_call x1, Pallas kernels, shards(): pl.pallas_call(late_kernel, out_shape=jax.ShapeDtypeStruct((late_count, l...  6.26 us
    pallas_call x1, Pallas kernels, shards(): pl.pallas_call(early_kernel, out_shape=[jax.ShapeDtypeStruct((early_count...  4.14 us
    pallas_call x2, Pallas kernels, terms(): pl.pallas_call(functools.partial(term_kernel, first, first_slot), out_sha...  4.14 us
    unnamed x14, local copies, waits for them, and re-layouts  3.19 us
  transfers between devices with their start and end apart: 2, of which 1 were waited for; matrix products, arithmetic and copies ran while one was open for 1% of the time, Pallas kernels for 13%

profile of v5, /device:TPU:1, one launch (start us, length us, event | category | flops | bytes accessed | tf_op | source)
XLA Modules:
  0.0 81.2 jit_solution(12768395247539492685)
XLA Ops:
  0.0 1.5 %request.1 = s32[16,128]{1,0:T(8,128)} custom-call(s32[1,11]{1,0:T(1,128)} %bitcast.18, s32[1,11]{1,0:T(1,128)} %bitcast.22, s32[1,11]{1,0:T(1,128)} %bitcast.23), custom_call_target="tpu_custom_call" | custom-call | tf_op jit(solution)/shard_map/request/pallas_call | solution.py:225
  1.5 7.6 %all-to-all-start = ((s32[16,1,128]{2,1,0:T(1,128)}), s32[16,1,128]{2,1,0:T(1,128)S(1)}, u32[]{:S(2)}, u32[]{:S(2)}) async-start(s32[16,1,128]{2,1,0:T(1,128)} %bitcast.21), calls=%async_computation | async-start | bytes 16384 | tf_op jit(solution)/shard_map/all_to_all | solution.py:232
  9.2 0.0 copy-start.1
  9.2 1.0 %copy-done.1 = bf16[32,52,52]{2,0,1:T(8,128)(2,1)S(1)} copy-done((bf16[32,52,52]{2,0,1:T(8,128)(2,1)S(1)}, bf16[32,52,52]{2,0,1:T(8,128)(2,1)}, u32[]{:S(2)}) %copy-start.1) | copy-done | bytes 173080
  10.2 0.0 copy-start.2
  10.2 0.8 %copy-done.2 = bf16[128,256]{1,0:T(8,128)(2,1)S(1)} copy-done((bf16[128,256]{1,0:T(8,128)(2,1)S(1)}, bf16[128,256]{1,0:T(8,128)(2,1)}, u32[]{:S(2)}) %copy-start.2) | copy-done | bytes 65560
  11.0 0.0 copy-start.4
  11.0 0.7 copy-done.4
  11.7 0.0 copy-start.6
  11.7 0.7 copy-done.6
  12.3 0.0 copy-start.5
  12.3 4.1 %early.1 = (bf16[3,1536,128]{2,1,0:T(8,128)(2,1)}, bf16[32,56,128]{2,1,0:T(8,128)(2,1)S(1)}, bf16[2,48,64]{2,1,0:T(8,128)(2,1)S(1)}) custom-call(s32[11]{0:T(128)S(1)} %copy-done.4, bf16[11,64,3328]{2,1,0:T(8,128)(2,1)} %tile_ref.3, bf16[52,32,52]{2,1,0:T(8,128)(2,1)S(1)} %bitcast.12, bf16[128,256]{1,0:T(8,128)(2,1)S(1)} %copy-done.2, s32[2,48]{1,0:T(2,128)S(1)} %copy-done.6), custom_call_target="tpu_custom_call" | custom-call | flops 61341696 | bytes 2457600 | tf_op jit(solution)/shard_map/early/pallas_call | solution.py:257
  16.5 0.0 all-to-all-done
  16.5 0.1 slice.24
  16.6 0.1 fusion.9
  16.6 0.1 slice.22
  16.7 1.4 %serve.1 = bf16[16,56,128]{2,1,0:T(8,128)(2,1)} custom-call(s32[16,128]{1,0:T(8,128)S(1)} %bitcast.16, bf16[32,56,128]{2,1,0:T(8,128)(2,1)S(1)} %get-tuple-element.12.metric_ref), custom_call_target="tpu_custom_call" | custom-call | tf_op jit(solution)/shard_map/serve/pallas_call | solution.py:276
  18.2 6.7 %all-to-all-start.1 = ((bf16[16,56,128]{2,1,0:T(8,128)(2,1)}), bf16[16,56,128]{2,1,0:T(8,128)(2,1)S(1)}, u32[]{:S(2)}, u32[]{:S(2)}) async-start(bf16[16,56,128]{2,1,0:T(8,128)(2,1)} %serve.1), calls=%async_computation.1 | async-start | bytes 458752 | tf_op jit(solution)/shard_map/all_to_all | solution.py:284
  24.8 0.0 copy-done.5
  24.8 0.0 copy-start.3
  24.8 6.3 %late.1.halves_ref = bf16[8,1536,128]{2,1,0:T(8,128)(2,1)S(1)} custom-call(s32[11]{0:T(128)S(1)} %copy-done.5, bf16[11,64,3328]{2,1,0:T(8,128)(2,1)} %tile_ref.3, bf16[2,48,64]{2,1,0:T(8,128)(2,1)S(1)} %get-tuple-element.14.picked_ref), custom_call_target="tpu_custom_call" | custom-call | flops 163577856 | bytes 6553600 | tf_op jit(solution)/shard_map/late/pallas_call | solution.py:287
  31.1 0.1 select_add_fusion
  31.2 0.1 eq.63
  31.3 0.1 eq.59
  31.4 0.2 select_convert_fusion.pick_ref
  31.6 0.4 all-to-all-done.1.metric_ref
  31.9 0.0 copy-start
  31.9 0.0 copy-done.3
  31.9 2.6 %late_term.1.refs_0_ = f32[512,128]{1,0:T(8,128)S(1)} custom-call(s32[11]{0:T(128)S(1)} %bitcast.19, bf16[8,1536,128]{2,1,0:T(8,128)(2,1)S(1)} %late.1.halves_ref, bf16[16,56,128]{2,1,0:T(8,128)(2,1)S(1)} %all-to-all-done.1.metric_ref), custom_call_target="tpu_custom_call" | custom-call | flops 603979776 | bytes 3145728 | tf_op jit(solution)/shard_map/late_term/pallas_call | solution.py:324
  34.6 0.0 copy-done
  34.6 1.5 %early_term.1 = bf16[512,128]{1,0:T(8,128)(2,1)S(1)} custom-call(s32[11]{0:T(128)S(1)} %bitcast.20, bf16[3,1536,128]{2,1,0:T(8,128)(2,1)S(1)} %copy-done, bf16[16,56,128]{2,1,0:T(8,128)(2,1)S(1)} %all-to-all-done.1.metric_ref, f32[512,128]{1,0:T(8,128)S(1)} %late_term.1.refs_0_), custom_call_target="tpu_custom_call" | custom-call | flops 226492416 | bytes 1179648 | tf_op jit(solution)/shard_map/early_term/pallas_call | solution.py:324
  36.1 12.8 %all_to_all.20.parts_ref = bf16[16,32,128]{2,1,0:T(8,128)(2,1)S(1)} all-to-all(bf16[16,32,128]{2,1,0:T(8,128)(2,1)S(1)} %bitcast.11), channel_id=1, replica_groups=mesh['pair'=32,'aux'=16] {'aux'}, dimensions={0} | all-to-all | bytes 262144 | tf_op jit(solution)/shard_map/all_to_all | solution.py:343
  48.9 0.3 combine.1
  49.2 31.3 %all_to_all.21.parts_ref = f32[32,4,128]{2,1,0:T(4,128)S(1)} all-to-all(f32[32,4,128]{2,1,0:T(4,128)S(1)} %bitcast.17), channel_id=1, replica_groups=mesh['pair'=32,'aux'=16] {'pair'}, dimensions={0} | all-to-all | bytes 131072 | tf_op jit(solution)/shard_map/all_to_all | solution.py:355
  80.5 0.7 final.1
  (5 shorter events, 0.0 us)
Async XLA Ops:
  1.5 15.0 %all-to-all-start = ((s32[16,1,128]{2,1,0:T(1,128)}), s32[16,1,128]{2,1,0:T(1,128)S(1)}, u32[]{:S(2)}, u32[]{:S(2)}) async-start(s32[16,1,128]{2,1,0:T(1,128)} %bitcast.21), calls=%async_computation | async-start | bytes 16384 | tf_op jit(solution)/shard_map/all_to_all | solution.py:232
  9.2 1.0 %copy-start.1 = (bf16[32,52,52]{2,0,1:T(8,128)(2,1)S(1)}, bf16[32,52,52]{2,0,1:T(8,128)(2,1)}, u32[]{:S(2)}) copy-start(bf16[32,52,52]{2,0,1:T(8,128)(2,1)} %param.15) | copy-start | bytes 519172
  10.2 0.8 %copy-start.2 = (bf16[128,256]{1,0:T(8,128)(2,1)S(1)}, bf16[128,256]{1,0:T(8,128)(2,1)}, u32[]{:S(2)}) copy-start(bf16[128,256]{1,0:T(8,128)(2,1)} %coeff_ref.1) | copy-start | bytes 196612
  11.0 0.7 copy-start.4
  11.7 0.7 copy-start.6
  12.3 12.5 %copy-start.5 = (s32[11]{0:T(128)S(1)}, s32[11]{0:T(128)}, u32[]{:S(2)}) copy-start(s32[11]{0:T(128)} %row_ref.3) | copy-start | bytes 136
  18.2 13.8 %all-to-all-start.1 = ((bf16[16,56,128]{2,1,0:T(8,128)(2,1)}), bf16[16,56,128]{2,1,0:T(8,128)(2,1)S(1)}, u32[]{:S(2)}, u32[]{:S(2)}) async-start(bf16[16,56,128]{2,1,0:T(8,128)(2,1)} %serve.1), calls=%async_computation.1 | async-start | bytes 458752 | tf_op jit(solution)/shard_map/all_to_all | solution.py:284
  24.8 7.1 %copy-start.3 = (s32[11,1]{0,1:T(1,128)S(1)}, s32[11,1]{0,1:T(1,128)}, u32[]{:S(2)}) copy-start(s32[11,1]{0,1:T(1,128)} %param.13) | copy-start | bytes 136
  31.9 2.6 %copy-start = (bf16[3,1536,128]{2,1,0:T(8,128)(2,1)S(1)}, bf16[3,1536,128]{2,1,0:T(8,128)(2,1)}, u32[]{:S(2)}) copy-start(bf16[3,1536,128]{2,1,0:T(8,128)(2,1)} %get-tuple-element.11.halves_ref) | copy-start | bytes 3538948

commit v6 on v5

--- a/solution.py
+++ b/solution.py
@@ -9,8 +9,9 @@
 LANES = 128
 HALF = 64
 MIB = 1 << 20
-EARLY_LIMIT = 55_200_000
-SERVE_LIMIT = 8 * MIB
+ROOM = 700
+EARLY_LIMIT = 61_000_000
+SERVE_LIMIT = 51_000_000
 LATE_LIMIT = 51_000_000
 TERM_LIMIT = 51_000_000
 SLOTS = 8
@@ -97,11 +98,18 @@
 
 
 def early_kernel(row_ref, tile_ref, metric_ref, coeff_ref, support_ref, *refs):
-    out_ref, padded_ref, picked_ref, rows_ref, made_ref, buffer_ref, half_ref, slab_ref, sems = refs
+    out_ref, padded_out, picked_out, padded_ref, picked_ref, rows_ref, made_ref, *refs = refs
+    buffer_ref, half_ref, slab_ref, sems = refs
     count = buffer_ref.shape[0]
     first = tile_ref.shape[0] - count
     copies = fetch(tile_ref, first, buffer_ref, sems)
     place(metric_ref, coeff_ref, support_ref, padded_ref, picked_ref, rows_ref)
+    placed = [
+        pltpu.make_async_copy(ref, out.at[pl.ds(0, ref.shape[0])], sems.at[2 * count + at])
+        for at, (ref, out) in enumerate(((padded_ref, padded_out), (picked_ref, picked_out)))
+    ]
+    for copy in placed:
+        copy.start()
     sends = [
         pltpu.make_async_copy(made_ref.at[item], out_ref.at[item], sems.at[count + item])
         for item in range(count)
@@ -113,12 +121,18 @@
             sends[item].start()
 
     half_tiles(row_ref, first, picked_ref, copies, buffer_ref, half_ref, slab_ref, put)
-    for send in sends:
-        send.wait()
-
-
-def late_kernel(row_ref, tile_ref, picked_ref, out_ref, buffer_ref, half_ref, slab_ref, sems):
+    for copy in sends + placed:
+        copy.wait()
+
+
+def late_kernel(row_ref, tile_ref, picked_in, out_ref, picked_ref, *refs):
+    buffer_ref, half_ref, slab_ref, sems = refs
+    picked_copy = pltpu.make_async_copy(
+        picked_in.at[pl.ds(0, picked_ref.shape[0])], picked_ref, sems.at[2 * buffer_ref.shape[0]]
+    )
+    picked_copy.start()
     copies = fetch(tile_ref, 0, buffer_ref, sems)
+    picked_copy.wait()
 
     def put(item, at, rows):
         out_ref[item, at : at + rows.shape[0], :] = rows
@@ -126,7 +140,10 @@
     half_tiles(row_ref, 0, picked_ref, copies, buffer_ref, half_ref, slab_ref, put)
 
 
-def serve_kernel(asked_ref, metric_ref, out_ref):
+def serve_kernel(asked_ref, metric_in, out_ref, metric_ref, sem):
+    copy = pltpu.make_async_copy(metric_in.at[pl.ds(0, metric_ref.shape[0])], metric_ref, sem)
+    copy.start()
+    copy.wait()
     lane = lax.broadcasted_iota(jnp.int32, out_ref.shape[1:], 1)
     for peer in range(out_ref.shape[0]):
         out_ref[peer] = jnp.where(
@@ -244,7 +261,7 @@
             pltpu.VMEM((count, width, columns), jnp.bfloat16),
             pltpu.VMEM((2, orbitals, columns), jnp.float32),
             pltpu.VMEM((2, late_rows, LANES), jnp.float32),
-            pltpu.SemaphoreType.DMA((2 * count,)),
+            pltpu.SemaphoreType.DMA((2 * count + 2,)),
         ]
 
     def cost(count):
@@ -254,16 +271,20 @@
             transcendentals=0,
         )
 
+    padded_shape = (metric.shape[0], depth, LANES)
+    picked_shape = (support.shape[0], orbitals, width)
     early, padded, picked = pl.pallas_call(
         early_kernel,
         out_shape=[
             jax.ShapeDtypeStruct((early_count, late_rows, LANES), jnp.bfloat16),
-            jax.ShapeDtypeStruct((metric.shape[0], depth, LANES), jnp.bfloat16),
-            jax.ShapeDtypeStruct((support.shape[0], orbitals, width), jnp.bfloat16),
+            jax.ShapeDtypeStruct((ROOM,) + padded_shape[1:], jnp.bfloat16),
+            jax.ShapeDtypeStruct((ROOM,) + picked_shape[1:], jnp.bfloat16),
         ],
         in_specs=[smem, anywhere, vmem, vmem, vmem],
-        out_specs=[anywhere, vmem, vmem],
+        out_specs=[anywhere] * 3,
         scratch_shapes=[
+            pltpu.VMEM(padded_shape, jnp.bfloat16),
+            pltpu.VMEM(picked_shape, jnp.bfloat16),
             pltpu.VMEM((aux_width * metric.shape[0], LANES), jnp.float32),
             pltpu.VMEM((early_count, late_rows, LANES), jnp.bfloat16),
         ]
@@ -276,8 +297,9 @@
     served = pl.pallas_call(
         serve_kernel,
         out_shape=jax.ShapeDtypeStruct((aux_count, depth, LANES), jnp.bfloat16),
-        in_specs=[smem, vmem],
+        in_specs=[smem, anywhere],
         out_specs=vmem,
+        scratch_shapes=[pltpu.VMEM(padded_shape, jnp.bfloat16), pltpu.SemaphoreType.DMA],
         compiler_params=pltpu.CompilerParams(vmem_limit_bytes=SERVE_LIMIT),
         name="serve",
     )(asked, padded)
@@ -287,9 +309,9 @@
     late = pl.pallas_call(
         late_kernel,
         out_shape=jax.ShapeDtypeStruct((late_count, late_rows, LANES), jnp.bfloat16),
-        in_specs=[smem, anywhere, vmem],
+        in_specs=[smem, anywhere, anywhere],
         out_specs=vmem,
-        scratch_shapes=half_scratch(late_count),
+        scratch_shapes=[pltpu.VMEM(picked_shape, jnp.bfloat16)] + half_scratch(late_count),
         compiler_params=pltpu.CompilerParams(vmem_limit_bytes=LATE_LIMIT),
         cost_estimate=cost(late_count),
         name="late",
@@ -329,7 +351,7 @@
             scratch_shapes=[pltpu.VMEM((width * SLOTS, LANES), jnp.float32)],
             compiler_params=pltpu.CompilerParams(vmem_limit_bytes=TERM_LIMIT),
             cost_estimate=pl.CostEstimate(
-                flops=2 * halves.shape[0] * late_rows * LANES * (LANES + width),
+                flops=12 * halves.shape[0] * late_rows * LANES * (LANES + width),
                 bytes_accessed=2 * halves.size,
                 transcendentals=0,
             ),

time: 81.7 us -> 80.1 us (0.980)
  local copies, waits for them, and re-layouts: 3.61 us -> 0.43 us
  waiting for transfers between devices: 0.36 us -> 1.99 us
  Pallas kernels: 18.5 us -> 20.1 us
  starting transfers between devices: 14.2 us -> 12.6 us
    unnamed x14 -> x6, local copies, waits for them, and re-layouts: 3.19 us -> 0.01 us
    all_to_all x1, waiting for transfers between devices: 0.01 us -> 1.67 us  [shards(): lax.all_to_all(request.reshape(aux_count, 1, LANES), 'aux', split_axis=0,...]
    all_to_all x1, starting transfers between devices: 6.65 us -> 5 us  [shards(): lax.all_to_all(served, 'aux', split_axis=0, concat_axis=0, tiled=True)]
    pallas_call x1, Pallas kernels: 1.44 us -> 2.46 us  [shards(): pl.pallas_call(serve_kernel, out_shape=jax.ShapeDtypeStruct((aux_count, d...]
  transfers between devices with their start and end apart: 2 -> 2, of which waited for: 1 -> 2; matrix products, arithmetic and copies ran while one was open for 1% -> 1% of each run, Pallas kernels for 13% -> 14%
where the time goes in v6:
time: 80.1 us; the launch traced here: 79.7 us
  blocking collectives  44.2 us (55%)
  Pallas kernels  20.1 us (25%)
  starting transfers between devices  12.6 us (16%)
  waiting for transfers between devices  1.99 us (2%)
    all_to_all x1, blocking collectives, shards(): lax.all_to_all(sums.reshape(pair_count, rows, LANES), 'pair', split_axis=...  31.3 us
    all_to_all x1, blocking collectives, shards(): lax.all_to_all(blocks.reshape(aux_count, rows * SLOTS, LANES), 'aux', spl...  12.9 us
    all_to_all x1, starting transfers between devices, shards(): lax.all_to_all(request.reshape(aux_count, 1, LANES), 'aux', split_axis=0,...  7.58 us
    pallas_call x1, Pallas kernels, shards(): pl.pallas_call(late_kernel, out_shape=jax.ShapeDtypeStruct((late_count, l...  6.29 us
    all_to_all x1, starting transfers between devices, shards(): lax.all_to_all(served, 'aux', split_axis=0, concat_axis=0, tiled=True)  5 us
    pallas_call x1, Pallas kernels, shards(): pl.pallas_call(early_kernel, out_shape=[jax.ShapeDtypeStruct((early_count...  4.7 us
    pallas_call x2, Pallas kernels, terms(): pl.pallas_call(functools.partial(term_kernel, first, first_slot), out_sha...  4.13 us
    pallas_call x1, Pallas kernels, shards(): pl.pallas_call(serve_kernel, out_shape=jax.ShapeDtypeStruct((aux_count, d...  2.46 us
  transfers between devices with their start and end apart: 2, of which 2 were waited for; matrix products, arithmetic and copies ran while one was open for 1% of the time, Pallas kernels for 14%

profile of v6, /device:TPU:1, one launch (start us, length us, event | category | flops | bytes accessed | tf_op | source)
XLA Modules:
  0.0 79.7 jit_solution(4001761635921558769)
XLA Ops:
  0.0 1.5 %request.1 = s32[16,128]{1,0:T(8,128)} custom-call(s32[1,11]{1,0:T(1,128)} %bitcast.17, s32[1,11]{1,0:T(1,128)} %bitcast.22, s32[1,11]{1,0:T(1,128)} %bitcast.23), custom_call_target="tpu_custom_call" | custom-call | tf_op jit(solution)/shard_map/request/pallas_call | solution.py:242
  1.5 7.6 %all-to-all-start = ((s32[16,1,128]{2,1,0:T(1,128)}), s32[16,1,128]{2,1,0:T(1,128)S(1)}, u32[]{:S(2)}, u32[]{:S(2)}) async-start(s32[16,1,128]{2,1,0:T(1,128)} %bitcast.21), calls=%async_computation | async-start | bytes 16384 | tf_op jit(solution)/shard_map/all_to_all | solution.py:249
  9.2 4.7 %early.1 = (bf16[3,1536,128]{2,1,0:T(8,128)(2,1)}, bf16[700,56,128]{2,1,0:T(8,128)(2,1)}, bf16[700,48,64]{2,1,0:T(8,128)(2,1)}) custom-call(s32[11]{0:T(128)} %row_ref.3, bf16[11,64,3328]{2,1,0:T(8,128)(2,1)} %tile_ref.3, bf16[52,32,52]{2,1,0:T(8,128)(2,1)} %bitcast.20, bf16[128,256]{1,0:T(8,128)(2,1)} %coeff_ref.1, s32[2,48]{1,0:T(2,128)} %support_ref.1), custom_call_target="tpu_custom_call" | custom-call | flops 61341696 | bytes 2457600 | tf_op jit(solution)/shard_map/early/pallas_call | solution.py:276
  13.9 1.7 %all-to-all-done = s32[16,1,128]{2,1,0:T(1,128)S(1)} async-done(((s32[16,1,128]{2,1,0:T(1,128)}), s32[16,1,128]{2,1,0:T(1,128)S(1)}, u32[]{:S(2)}, u32[]{:S(2)}) %all-to-all-start) | async-done | bytes 8224 | tf_op jit(solution)/shard_map/all_to_all | solution.py:249
  15.5 0.1 slice.24
  15.6 0.1 fusion.9
  15.7 0.1 slice.22
  15.8 0.0 copy-start
  15.8 2.5 %serve.1 = bf16[16,56,128]{2,1,0:T(8,128)(2,1)} custom-call(s32[16,128]{1,0:T(8,128)S(1)} %bitcast.14, bf16[700,56,128]{2,1,0:T(8,128)(2,1)} %get-tuple-element.12.metric_in), custom_call_target="tpu_custom_call" | custom-call | tf_op jit(solution)/shard_map/serve/pallas_call | solution.py:297
  18.2 5.0 %all-to-all-start.1 = ((bf16[16,56,128]{2,1,0:T(8,128)(2,1)}), bf16[16,56,128]{2,1,0:T(8,128)(2,1)S(1)}, u32[]{:S(2)}, u32[]{:S(2)}) async-start(bf16[16,56,128]{2,1,0:T(8,128)(2,1)} %serve.1), calls=%async_computation.1 | async-start | bytes 458752 | tf_op jit(solution)/shard_map/all_to_all | solution.py:306
  23.2 0.0 copy-done
  23.2 0.0 copy-start.1
  23.3 6.3 %late.1.halves_ref = bf16[8,1536,128]{2,1,0:T(8,128)(2,1)S(1)} custom-call(s32[11]{0:T(128)S(1)} %copy-done, bf16[11,64,3328]{2,1,0:T(8,128)(2,1)} %tile_ref.3, bf16[700,48,64]{2,1,0:T(8,128)(2,1)} %get-tuple-element.14.picked_in), custom_call_target="tpu_custom_call" | custom-call | flops 163577856 | bytes 6553600 | tf_op jit(solution)/shard_map/late/pallas_call | solution.py:309
  29.6 0.1 select_add_fusion
  29.6 0.1 eq.63
  29.8 0.1 eq.59
  29.9 0.2 select_convert_fusion.pick_ref
  30.0 0.3 all-to-all-done.1.metric_ref
  30.4 0.0 copy-done.1
  30.4 0.0 copy-start.2
  30.4 2.6 %late_term.1.refs_0_ = f32[512,128]{1,0:T(8,128)S(1)} custom-call(s32[11]{0:T(128)S(1)} %bitcast.18, bf16[8,1536,128]{2,1,0:T(8,128)(2,1)S(1)} %late.1.halves_ref, bf16[16,56,128]{2,1,0:T(8,128)(2,1)S(1)} %all-to-all-done.1.metric_ref), custom_call_target="tpu_custom_call" | custom-call | flops 3623878656 | bytes 3145728 | tf_op jit(solution)/shard_map/late_term/pallas_call | solution.py:346
  33.0 0.0 copy-done.2
  33.0 1.5 %early_term.1 = bf16[512,128]{1,0:T(8,128)(2,1)S(1)} custom-call(s32[11]{0:T(128)S(1)} %bitcast.19, bf16[3,1536,128]{2,1,0:T(8,128)(2,1)S(1)} %copy-done.2, bf16[16,56,128]{2,1,0:T(8,128)(2,1)S(1)} %all-to-all-done.1.metric_ref, f32[512,128]{1,0:T(8,128)S(1)} %late_term.1.refs_0_), custom_call_target="tpu_custom_call" | custom-call | flops 1358954496 | bytes 1179648 | tf_op jit(solution)/shard_map/early_term/pallas_call | solution.py:346
  34.5 12.9 %all_to_all.20.parts_ref = bf16[16,32,128]{2,1,0:T(8,128)(2,1)S(1)} all-to-all(bf16[16,32,128]{2,1,0:T(8,128)(2,1)S(1)} %bitcast.16), channel_id=1, replica_groups=mesh['pair'=32,'aux'=16] {'aux'}, dimensions={0} | all-to-all | bytes 262144 | tf_op jit(solution)/shard_map/all_to_all | solution.py:365
  47.4 0.3 combine.1
  47.6 31.3 %all_to_all.21.parts_ref = f32[32,4,128]{2,1,0:T(4,128)S(1)} all-to-all(f32[32,4,128]{2,1,0:T(4,128)S(1)} %bitcast.15), channel_id=1, replica_groups=mesh['pair'=32,'aux'=16] {'pair'}, dimensions={0} | all-to-all | bytes 131072 | tf_op jit(solution)/shard_map/all_to_all | solution.py:377
  79.0 0.7 final.1
  (5 shorter events, 0.0 us)
Async XLA Ops:
  1.5 14.0 %all-to-all-start = ((s32[16,1,128]{2,1,0:T(1,128)}), s32[16,1,128]{2,1,0:T(1,128)S(1)}, u32[]{:S(2)}, u32[]{:S(2)}) async-start(s32[16,1,128]{2,1,0:T(1,128)} %bitcast.21), calls=%async_computation | async-start | bytes 16384 | tf_op jit(solution)/shard_map/all_to_all | solution.py:249
  15.8 7.5 %copy-start = (s32[11]{0:T(128)S(1)}, s32[11]{0:T(128)}, u32[]{:S(2)}) copy-start(s32[11]{0:T(128)} %row_ref.3) | copy-start | bytes 136
  18.2 12.1 %all-to-all-start.1 = ((bf16[16,56,128]{2,1,0:T(8,128)(2,1)}), bf16[16,56,128]{2,1,0:T(8,128)(2,1)S(1)}, u32[]{:S(2)}, u32[]{:S(2)}) async-start(bf16[16,56,128]{2,1,0:T(8,128)(2,1)} %serve.1), calls=%async_computation.1 | async-start | bytes 458752 | tf_op jit(solution)/shard_map/all_to_all | solution.py:306
  23.2 7.1 %copy-start.1 = (s32[11,1]{0,1:T(1,128)S(1)}, s32[11,1]{0,1:T(1,128)}, u32[]{:S(2)}) copy-start(s32[11,1]{0,1:T(1,128)} %param.13) | copy-start | bytes 136
  30.4 2.6 %copy-start.2 = (bf16[3,1536,128]{2,1,0:T(8,128)(2,1)S(1)}, bf16[3,1536,128]{2,1,0:T(8,128)(2,1)}, u32[]{:S(2)}) copy-start(bf16[3,1536,128]{2,1,0:T(8,128)(2,1)} %get-tuple-element.11.halves_ref) | copy-start | bytes 3538948

commit v7 on v6

--- a/solution.py
+++ b/solution.py
@@ -11,7 +11,7 @@
 MIB = 1 << 20
 ROOM = 700
 EARLY_LIMIT = 61_000_000
-SERVE_LIMIT = 51_000_000
+STAGE_LIMIT = 51_000_000
 LATE_LIMIT = 51_000_000
 TERM_LIMIT = 51_000_000
 SLOTS = 8
@@ -140,10 +140,13 @@
     half_tiles(row_ref, 0, picked_ref, copies, buffer_ref, half_ref, slab_ref, put)
 
 
-def serve_kernel(asked_ref, metric_in, out_ref, metric_ref, sem):
+def stage_kernel(metric_in, metric_ref, sem):
     copy = pltpu.make_async_copy(metric_in.at[pl.ds(0, metric_ref.shape[0])], metric_ref, sem)
     copy.start()
     copy.wait()
+
+
+def serve_kernel(asked_ref, metric_ref, out_ref):
     lane = lax.broadcasted_iota(jnp.int32, out_ref.shape[1:], 1)
     for peer in range(out_ref.shape[0]):
         out_ref[peer] = jnp.where(
@@ -294,13 +297,22 @@
         name="early",
     )(row_block, tiles, by_aux, coeff, support)
 
+    padded = pl.pallas_call(
+        stage_kernel,
+        out_shape=jax.ShapeDtypeStruct(padded_shape, jnp.bfloat16),
+        in_specs=[anywhere],
+        out_specs=vmem,
+        scratch_shapes=[pltpu.SemaphoreType.DMA],
+        compiler_params=pltpu.CompilerParams(vmem_limit_bytes=STAGE_LIMIT),
+        name="stage",
+    )(padded)
+
     served = pl.pallas_call(
         serve_kernel,
         out_shape=jax.ShapeDtypeStruct((aux_count, depth, LANES), jnp.bfloat16),
-        in_specs=[smem, anywhere],
-        out_specs=vmem,
-        scratch_shapes=[pltpu.VMEM(padded_shape, jnp.bfloat16), pltpu.SemaphoreType.DMA],
-        compiler_params=pltpu.CompilerParams(vmem_limit_bytes=SERVE_LIMIT),
+        in_specs=[smem, vmem],
+        out_specs=vmem,
+        compiler_params=pltpu.CompilerParams(vmem_limit_bytes=8 * MIB),
         name="serve",
     )(asked, padded)
     metric_tiles = lax.all_to_all(served, "aux", split_axis=0, concat_axis=0, tiled=True)

time: 80.1 us -> 80 us (level)
  waiting for transfers between devices: 1.99 us -> 0.93 us
  starting transfers between devices: 12.6 us -> 13.6 us
    all_to_all x1, waiting for transfers between devices: 1.67 us -> 0.61 us  [shards(): lax.all_to_all(request.reshape(aux_count, 1, LANES), 'aux', split_axis=0,...]
    all_to_all x1, starting transfers between devices: 5 us -> 6.05 us  [shards(): lax.all_to_all(served, 'aux', split_axis=0, concat_axis=0, tiled=True)]
    pallas_call x0 -> x1, Pallas kernels: none -> 1.03 us  [shards(): pl.pallas_call(stage_kernel, out_shape=jax.ShapeDtypeStruct(padded_shape,...]
    pallas_call x1, Pallas kernels: 2.46 us -> 1.43 us  [shards(): pl.pallas_call(serve_kernel, out_shape=jax.ShapeDtypeStruct((aux_count, d...]
  transfers between devices with their start and end apart: 2 -> 2, of which waited for: 2 -> 2; matrix products, arithmetic and copies ran while one was open for 1% -> 1% of each run, Pallas kernels for 14% -> 15%
where the time goes in v7:
time: 80 us; the launch traced here: 79.7 us
  blocking collectives  44.2 us (55%)
  Pallas kernels  20.1 us (25%)
  starting transfers between devices  13.6 us (17%)
  waiting for transfers between devices  0.93 us (1%)
    all_to_all x1, blocking collectives, shards(): lax.all_to_all(sums.reshape(pair_count, rows, LANES), 'pair', split_axis=...  31.3 us
    all_to_all x1, blocking collectives, shards(): lax.all_to_all(blocks.reshape(aux_count, rows * SLOTS, LANES), 'aux', spl...  12.9 us
    all_to_all x1, starting transfers between devices, shards(): lax.all_to_all(request.reshape(aux_count, 1, LANES), 'aux', split_axis=0,...  7.58 us
    pallas_call x1, Pallas kernels, shards(): pl.pallas_call(late_kernel, out_shape=jax.ShapeDtypeStruct((late_count, l...  6.29 us
    all_to_all x1, starting transfers between devices, shards(): lax.all_to_all(served, 'aux', split_axis=0, concat_axis=0, tiled=True)  6.05 us
    pallas_call x1, Pallas kernels, shards(): pl.pallas_call(early_kernel, out_shape=[jax.ShapeDtypeStruct((early_count...  4.7 us
    pallas_call x2, Pallas kernels, terms(): pl.pallas_call(functools.partial(term_kernel, first, first_slot), out_sha...  4.13 us
  transfers between devices with their start and end apart: 2, of which 2 were waited for; matrix products, arithmetic and copies ran while one was open for 1% of the time, Pallas kernels for 15%

profile of v7, /device:TPU:1, one launch (start us, length us, event | category | flops | bytes accessed | tf_op | source)
XLA Modules:
  0.0 79.7 jit_solution(16824769072901853649)
XLA Ops:
  0.0 1.5 %request.1 = s32[16,128]{1,0:T(8,128)} custom-call(s32[1,11]{1,0:T(1,128)} %bitcast.17, s32[1,11]{1,0:T(1,128)} %bitcast.22, s32[1,11]{1,0:T(1,128)} %bitcast.23), custom_call_target="tpu_custom_call" | custom-call | tf_op jit(solution)/shard_map/request/pallas_call | solution.py:245
  1.5 7.6 %all-to-all-start = ((s32[16,1,128]{2,1,0:T(1,128)}), s32[16,1,128]{2,1,0:T(1,128)S(1)}, u32[]{:S(2)}, u32[]{:S(2)}) async-start(s32[16,1,128]{2,1,0:T(1,128)} %bitcast.21), calls=%async_computation | async-start | bytes 16384 | tf_op jit(solution)/shard_map/all_to_all | solution.py:252
  9.2 4.7 %early.1 = (bf16[3,1536,128]{2,1,0:T(8,128)(2,1)}, bf16[700,56,128]{2,1,0:T(8,128)(2,1)}, bf16[700,48,64]{2,1,0:T(8,128)(2,1)}) custom-call(s32[11]{0:T(128)} %row_ref.3, bf16[11,64,3328]{2,1,0:T(8,128)(2,1)} %tile_ref.3, bf16[52,32,52]{2,1,0:T(8,128)(2,1)} %bitcast.20, bf16[128,256]{1,0:T(8,128)(2,1)} %coeff_ref.1, s32[2,48]{1,0:T(2,128)} %support_ref.1), custom_call_target="tpu_custom_call" | custom-call | flops 61341696 | bytes 2457600 | tf_op jit(solution)/shard_map/early/pallas_call | solution.py:279
  13.9 0.0 copy-start
  13.9 1.0 %stage.1.metric_ref = bf16[32,56,128]{2,1,0:T(8,128)(2,1)S(1)} custom-call(bf16[700,56,128]{2,1,0:T(8,128)(2,1)} %get-tuple-element.12.metric_in), custom_call_target="tpu_custom_call" | custom-call | tf_op jit(solution)/shard_map/stage/pallas_call | solution.py:300
  14.9 0.6 all-to-all-done
  15.5 0.1 slice.24
  15.6 0.1 fusion.9
  15.7 0.1 slice.22
  15.8 1.4 %serve.1 = bf16[16,56,128]{2,1,0:T(8,128)(2,1)} custom-call(s32[16,128]{1,0:T(8,128)S(1)} %bitcast.14, bf16[32,56,128]{2,1,0:T(8,128)(2,1)S(1)} %stage.1.metric_ref), custom_call_target="tpu_custom_call" | custom-call | tf_op jit(solution)/shard_map/serve/pallas_call | solution.py:310
  17.2 6.0 %all-to-all-start.1 = ((bf16[16,56,128]{2,1,0:T(8,128)(2,1)}), bf16[16,56,128]{2,1,0:T(8,128)(2,1)S(1)}, u32[]{:S(2)}, u32[]{:S(2)}) async-start(bf16[16,56,128]{2,1,0:T(8,128)(2,1)} %serve.1), calls=%async_computation.1 | async-start | bytes 458752 | tf_op jit(solution)/shard_map/all_to_all | solution.py:318
  23.2 0.0 copy-done
  23.2 0.0 copy-start.1
  23.3 6.3 %late.1.halves_ref = bf16[8,1536,128]{2,1,0:T(8,128)(2,1)S(1)} custom-call(s32[11]{0:T(128)S(1)} %copy-done, bf16[11,64,3328]{2,1,0:T(8,128)(2,1)} %tile_ref.3, bf16[700,48,64]{2,1,0:T(8,128)(2,1)} %get-tuple-element.14.picked_in), custom_call_target="tpu_custom_call" | custom-call | flops 163577856 | bytes 6553600 | tf_op jit(solution)/shard_map/late/pallas_call | solution.py:321
  29.6 0.1 select_add_fusion
  29.6 0.1 eq.63
  29.8 0.1 eq.59
  29.9 0.2 select_convert_fusion.pick_ref
  30.0 0.3 all-to-all-done.1.metric_ref
  30.4 0.0 copy-done.1
  30.4 0.0 copy-start.2
  30.4 2.6 %late_term.1.refs_0_ = f32[512,128]{1,0:T(8,128)S(1)} custom-call(s32[11]{0:T(128)S(1)} %bitcast.18, bf16[8,1536,128]{2,1,0:T(8,128)(2,1)S(1)} %late.1.halves_ref, bf16[16,56,128]{2,1,0:T(8,128)(2,1)S(1)} %all-to-all-done.1.metric_ref), custom_call_target="tpu_custom_call" | custom-call | flops 3623878656 | bytes 3145728 | tf_op jit(solution)/shard_map/late_term/pallas_call | solution.py:358
  33.0 0.0 copy-done.2
  33.0 1.5 %early_term.1 = bf16[512,128]{1,0:T(8,128)(2,1)S(1)} custom-call(s32[11]{0:T(128)S(1)} %bitcast.19, bf16[3,1536,128]{2,1,0:T(8,128)(2,1)S(1)} %copy-done.2, bf16[16,56,128]{2,1,0:T(8,128)(2,1)S(1)} %all-to-all-done.1.metric_ref, f32[512,128]{1,0:T(8,128)S(1)} %late_term.1.refs_0_), custom_call_target="tpu_custom_call" | custom-call | flops 1358954496 | bytes 1179648 | tf_op jit(solution)/shard_map/early_term/pallas_call | solution.py:358
  34.5 12.9 %all_to_all.20.parts_ref = bf16[16,32,128]{2,1,0:T(8,128)(2,1)S(1)} all-to-all(bf16[16,32,128]{2,1,0:T(8,128)(2,1)S(1)} %bitcast.16), channel_id=1, replica_groups=mesh['pair'=32,'aux'=16] {'aux'}, dimensions={0} | all-to-all | bytes 262144 | tf_op jit(solution)/shard_map/all_to_all | solution.py:377
  47.4 0.3 combine.1
  47.7 31.3 %all_to_all.21.parts_ref = f32[32,4,128]{2,1,0:T(4,128)S(1)} all-to-all(f32[32,4,128]{2,1,0:T(4,128)S(1)} %bitcast.15), channel_id=1, replica_groups=mesh['pair'=32,'aux'=16] {'pair'}, dimensions={0} | all-to-all | bytes 131072 | tf_op jit(solution)/shard_map/all_to_all | solution.py:389
  79.0 0.7 final.1
  (5 shorter events, 0.0 us)
Async XLA Ops:
  1.5 14.0 %all-to-all-start = ((s32[16,1,128]{2,1,0:T(1,128)}), s32[16,1,128]{2,1,0:T(1,128)S(1)}, u32[]{:S(2)}, u32[]{:S(2)}) async-start(s32[16,1,128]{2,1,0:T(1,128)} %bitcast.21), calls=%async_computation | async-start | bytes 16384 | tf_op jit(solution)/shard_map/all_to_all | solution.py:252
  13.9 9.4 %copy-start = (s32[11]{0:T(128)S(1)}, s32[11]{0:T(128)}, u32[]{:S(2)}) copy-start(s32[11]{0:T(128)} %row_ref.3) | copy-start | bytes 136
  17.2 13.2 %all-to-all-start.1 = ((bf16[16,56,128]{2,1,0:T(8,128)(2,1)}), bf16[16,56,128]{2,1,0:T(8,128)(2,1)S(1)}, u32[]{:S(2)}, u32[]{:S(2)}) async-start(bf16[16,56,128]{2,1,0:T(8,128)(2,1)} %serve.1), calls=%async_computation.1 | async-start | bytes 458752 | tf_op jit(solution)/shard_map/all_to_all | solution.py:318
  23.2 7.1 %copy-start.1 = (s32[11,1]{0,1:T(1,128)S(1)}, s32[11,1]{0,1:T(1,128)}, u32[]{:S(2)}) copy-start(s32[11,1]{0,1:T(1,128)} %param.13) | copy-start | bytes 136
  30.4 2.6 %copy-start.2 = (bf16[3,1536,128]{2,1,0:T(8,128)(2,1)S(1)}, bf16[3,1536,128]{2,1,0:T(8,128)(2,1)}, u32[]{:S(2)}) copy-start(bf16[3,1536,128]{2,1,0:T(8,128)(2,1)} %get-tuple-element.11.halves_ref) | copy-start | bytes 3538948

commit v8 on v7

--- a/solution.py
+++ b/solution.py
@@ -201,7 +201,7 @@
     out_ref[...] = total[...].astype(out_ref.dtype)
 
 
-def combine_kernel(parts_ref, pick_ref, out_ref):
+def combine_kernel(parts_ref, pick_ref, out_ref, sum_ref):
     sources = parts_ref.shape[0]
     rows = parts_ref.shape[1] // SLOTS
     pairs = pick_ref.shape[0] // 8
@@ -219,12 +219,18 @@
             odd = summed[at + 3 * pairs : at + 4 * pairs] + pltpu.roll(
                 summed[at + 2 * pairs : at + 3 * pairs], HALF, 1
             )
-            out_ref[pl.ds(step * 2 + parity, pairs, stride=rows), :] = jnp.where(low, even, odd)
+            sum_ref[pl.ds(step * 2 + parity, pairs, stride=rows), :] = jnp.where(low, even, odd)
+    out_ref[...] = sum_ref[...].astype(out_ref.dtype)
 
 
 def final_kernel(parts_ref, out_ref):
     rows = out_ref.shape[1]
-    summed = jnp.sum(parts_ref[...], axis=0)
+    parts = parts_ref[...].astype(jnp.float32)
+    step = 8 // rows * rows
+    summed = parts[:step]
+    for at in range(step, parts.shape[0], step):
+        summed = summed + parts[at : at + step]
+    summed = sum(summed[at : at + rows] for at in range(0, step, rows))
     for side in range(out_ref.shape[0]):
         out_ref[side] = summed[:, side * HALF : (side + 1) * HALF]
 
@@ -380,9 +386,10 @@
 
     sums = pl.pallas_call(
         combine_kernel,
-        out_shape=jax.ShapeDtypeStruct((pair_count * rows, LANES), jnp.float32),
+        out_shape=jax.ShapeDtypeStruct((pair_count * rows, LANES), jnp.bfloat16),
         in_specs=[vmem] * 2,
         out_specs=vmem,
+        scratch_shapes=[pltpu.VMEM((pair_count * rows, LANES), jnp.float32)],
         compiler_params=small,
         name="combine",
     )(parts, pick)
@@ -396,7 +403,7 @@
         out_specs=vmem,
         compiler_params=small,
         name="final",
-    )(arrived)
+    )(arrived.reshape(pair_count * rows, LANES))
 
 
 def solution(mesh):

time: 80 us -> 79.1 us (0.989)
  blocking collectives: 44.2 us -> 43.2 us
    all_to_all x1, blocking collectives: 31.3 us -> 30.4 us  [shards(): lax.all_to_all(sums.reshape(pair_count, rows, LANES), 'pair', split_axis=...]
where the time goes in v8:
time: 79.1 us; the launch traced here: 78.7 us
  blocking collectives  43.2 us (55%)
  Pallas kernels  20.1 us (25%)
  starting transfers between devices  13.6 us (17%)
  waiting for transfers between devices  0.94 us (1%)
    all_to_all x1, blocking collectives, shards(): lax.all_to_all(sums.reshape(pair_count, rows, LANES), 'pair', split_axis=...  30.4 us
    all_to_all x1, blocking collectives, shards(): lax.all_to_all(blocks.reshape(aux_count, rows * SLOTS, LANES), 'aux', spl...  12.8 us
    all_to_all x1, starting transfers between devices, shards(): lax.all_to_all(request.reshape(aux_count, 1, LANES), 'aux', split_axis=0,...  7.58 us
    pallas_call x1, Pallas kernels, shards(): pl.pallas_call(late_kernel, out_shape=jax.ShapeDtypeStruct((late_count, l...  6.28 us
    all_to_all x1, starting transfers between devices, shards(): lax.all_to_all(served, 'aux', split_axis=0, concat_axis=0, tiled=True)  6.05 us
    pallas_call x1, Pallas kernels, shards(): pl.pallas_call(early_kernel, out_shape=[jax.ShapeDtypeStruct((early_count...  4.7 us
    pallas_call x2, Pallas kernels, terms(): pl.pallas_call(functools.partial(term_kernel, first, first_slot), out_sha...  4.14 us
  transfers between devices with their start and end apart: 2, of which 2 were waited for; matrix products, arithmetic and copies ran while one was open for 1% of the time, Pallas kernels for 15%

profile of v8, /device:TPU:1, one launch (start us, length us, event | category | flops | bytes accessed | tf_op | source)
XLA Modules:
  0.0 78.7 jit_solution(6546170111232182690)
XLA Ops:
  0.0 1.5 %request.1 = s32[16,128]{1,0:T(8,128)} custom-call(s32[1,11]{1,0:T(1,128)} %bitcast.19, s32[1,11]{1,0:T(1,128)} %bitcast.24, s32[1,11]{1,0:T(1,128)} %bitcast.25), custom_call_target="tpu_custom_call" | custom-call | tf_op jit(solution)/shard_map/request/pallas_call | solution.py:251
  1.5 7.6 %all-to-all-start = ((s32[16,1,128]{2,1,0:T(1,128)}), s32[16,1,128]{2,1,0:T(1,128)S(1)}, u32[]{:S(2)}, u32[]{:S(2)}) async-start(s32[16,1,128]{2,1,0:T(1,128)} %bitcast.23), calls=%async_computation | async-start | bytes 16384 | tf_op jit(solution)/shard_map/all_to_all | solution.py:258
  9.2 4.7 %early.1 = (bf16[3,1536,128]{2,1,0:T(8,128)(2,1)}, bf16[700,56,128]{2,1,0:T(8,128)(2,1)}, bf16[700,48,64]{2,1,0:T(8,128)(2,1)}) custom-call(s32[11]{0:T(128)} %row_ref.3, bf16[11,64,3328]{2,1,0:T(8,128)(2,1)} %tile_ref.3, bf16[52,32,52]{2,1,0:T(8,128)(2,1)} %bitcast.22, bf16[128,256]{1,0:T(8,128)(2,1)} %coeff_ref.1, s32[2,48]{1,0:T(2,128)} %support_ref.1), custom_call_target="tpu_custom_call" | custom-call | flops 61341696 | bytes 2457600 | tf_op jit(solution)/shard_map/early/pallas_call | solution.py:285
  13.9 0.0 copy-start
  13.9 1.0 %stage.1.metric_ref = bf16[32,56,128]{2,1,0:T(8,128)(2,1)S(1)} custom-call(bf16[700,56,128]{2,1,0:T(8,128)(2,1)} %get-tuple-element.12.metric_in), custom_call_target="tpu_custom_call" | custom-call | tf_op jit(solution)/shard_map/stage/pallas_call | solution.py:306
  14.9 0.6 all-to-all-done
  15.5 0.1 slice.24
  15.6 0.1 fusion.9
  15.7 0.1 slice.22
  15.8 1.4 %serve.1 = bf16[16,56,128]{2,1,0:T(8,128)(2,1)} custom-call(s32[16,128]{1,0:T(8,128)S(1)} %bitcast.15, bf16[32,56,128]{2,1,0:T(8,128)(2,1)S(1)} %stage.1.metric_ref), custom_call_target="tpu_custom_call" | custom-call | tf_op jit(solution)/shard_map/serve/pallas_call | solution.py:316
  17.2 6.0 %all-to-all-start.1 = ((bf16[16,56,128]{2,1,0:T(8,128)(2,1)}), bf16[16,56,128]{2,1,0:T(8,128)(2,1)S(1)}, u32[]{:S(2)}, u32[]{:S(2)}) async-start(bf16[16,56,128]{2,1,0:T(8,128)(2,1)} %serve.1), calls=%async_computation.1 | async-start | bytes 458752 | tf_op jit(solution)/shard_map/all_to_all | solution.py:324
  23.2 0.0 copy-done
  23.2 0.0 copy-start.1
  23.3 6.3 %late.1.halves_ref = bf16[8,1536,128]{2,1,0:T(8,128)(2,1)S(1)} custom-call(s32[11]{0:T(128)S(1)} %copy-done, bf16[11,64,3328]{2,1,0:T(8,128)(2,1)} %tile_ref.3, bf16[700,48,64]{2,1,0:T(8,128)(2,1)} %get-tuple-element.14.picked_in), custom_call_target="tpu_custom_call" | custom-call | flops 163577856 | bytes 6553600 | tf_op jit(solution)/shard_map/late/pallas_call | solution.py:327
  29.6 0.1 select_add_fusion
  29.6 0.1 eq.63
  29.8 0.1 eq.59
  29.9 0.2 select_convert_fusion.pick_ref
  30.0 0.3 all-to-all-done.1.metric_ref
  30.4 0.0 copy-done.1
  30.4 0.0 copy-start.2
  30.4 2.6 %late_term.1.refs_0_ = f32[512,128]{1,0:T(8,128)S(1)} custom-call(s32[11]{0:T(128)S(1)} %bitcast.20, bf16[8,1536,128]{2,1,0:T(8,128)(2,1)S(1)} %late.1.halves_ref, bf16[16,56,128]{2,1,0:T(8,128)(2,1)S(1)} %all-to-all-done.1.metric_ref), custom_call_target="tpu_custom_call" | custom-call | flops 3623878656 | bytes 3145728 | tf_op jit(solution)/shard_map/late_term/pallas_call | solution.py:364
  33.0 0.0 copy-done.2
  33.0 1.5 %early_term.1 = bf16[512,128]{1,0:T(8,128)(2,1)S(1)} custom-call(s32[11]{0:T(128)S(1)} %bitcast.21, bf16[3,1536,128]{2,1,0:T(8,128)(2,1)S(1)} %copy-done.2, bf16[16,56,128]{2,1,0:T(8,128)(2,1)S(1)} %all-to-all-done.1.metric_ref, f32[512,128]{1,0:T(8,128)S(1)} %late_term.1.refs_0_), custom_call_target="tpu_custom_call" | custom-call | flops 1358954496 | bytes 1179648 | tf_op jit(solution)/shard_map/early_term/pallas_call | solution.py:364
  34.5 12.8 %all_to_all.20.parts_ref = bf16[16,32,128]{2,1,0:T(8,128)(2,1)S(1)} all-to-all(bf16[16,32,128]{2,1,0:T(8,128)(2,1)S(1)} %bitcast.17), channel_id=1, replica_groups=mesh['pair'=32,'aux'=16] {'aux'}, dimensions={0} | all-to-all | bytes 262144 | tf_op jit(solution)/shard_map/all_to_all | solution.py:383
  47.4 0.3 combine.1
  47.7 30.4 %all_to_all.21 = bf16[32,4,128]{2,1,0:T(4,128)(2,1)S(1)} all-to-all(bf16[32,4,128]{2,1,0:T(4,128)(2,1)S(1)} %bitcast.16), channel_id=1, replica_groups=mesh['pair'=32,'aux'=16] {'pair'}, dimensions={0} | all-to-all | bytes 65536 | tf_op jit(solution)/shard_map/all_to_all | solution.py:396
  78.0 0.7 final.1
  (5 shorter events, 0.0 us)
Async XLA Ops:
  1.5 14.0 %all-to-all-start = ((s32[16,1,128]{2,1,0:T(1,128)}), s32[16,1,128]{2,1,0:T(1,128)S(1)}, u32[]{:S(2)}, u32[]{:S(2)}) async-start(s32[16,1,128]{2,1,0:T(1,128)} %bitcast.23), calls=%async_computation | async-start | bytes 16384 | tf_op jit(solution)/shard_map/all_to_all | solution.py:258
  13.9 9.4 %copy-start = (s32[11]{0:T(128)S(1)}, s32[11]{0:T(128)}, u32[]{:S(2)}) copy-start(s32[11]{0:T(128)} %row_ref.3) | copy-start | bytes 136
  17.2 13.2 %all-to-all-start.1 = ((bf16[16,56,128]{2,1,0:T(8,128)(2,1)}), bf16[16,56,128]{2,1,0:T(8,128)(2,1)S(1)}, u32[]{:S(2)}, u32[]{:S(2)}) async-start(bf16[16,56,128]{2,1,0:T(8,128)(2,1)} %serve.1), calls=%async_computation.1 | async-start | bytes 458752 | tf_op jit(solution)/shard_map/all_to_all | solution.py:324
  23.2 7.1 %copy-start.1 = (s32[11,1]{0,1:T(1,128)S(1)}, s32[11,1]{0,1:T(1,128)}, u32[]{:S(2)}) copy-start(s32[11,1]{0,1:T(1,128)} %param.13) | copy-start | bytes 136
  30.4 2.6 %copy-start.2 = (bf16[3,1536,128]{2,1,0:T(8,128)(2,1)S(1)}, bf16[3,1536,128]{2,1,0:T(8,128)(2,1)}, u32[]{:S(2)}) copy-start(bf16[3,1536,128]{2,1,0:T(8,128)(2,1)} %get-tuple-element.11.halves_ref) | copy-start | bytes 3538948

commit v9 on v8

--- a/solution.py
+++ b/solution.py
@@ -11,7 +11,7 @@
 MIB = 1 << 20
 ROOM = 700
 EARLY_LIMIT = 61_000_000
-STAGE_LIMIT = 51_000_000
+TILES_LIMIT = 55_400_000
 LATE_LIMIT = 51_000_000
 TERM_LIMIT = 51_000_000
 SLOTS = 8
@@ -62,7 +62,7 @@
     return copies
 
 
-def half_tiles(row_ref, first, picked_ref, copies, buffer_ref, half_ref, slab_ref, put):
+def half_tiles(picked_ref, copies, buffer_ref, half_ref, slab_ref, put):
     item_count, width, columns = buffer_ref.shape
     orbitals = picked_ref.shape[1]
     groups = orbitals // 2
@@ -73,7 +73,7 @@
     def multiply(item):
         copies[item].wait()
         half_ref[item % 2] = jnp.dot(
-            picked_ref[row_ref[first + item]], buffer_ref[item], preferred_element_type=jnp.float32
+            picked_ref[item], buffer_ref[item], preferred_element_type=jnp.float32
         )
 
     multiply(0)
@@ -97,19 +97,26 @@
             put(item, g * width, slabs[pl.ds(g, width, stride=groups), :].astype(jnp.bfloat16))
 
 
-def early_kernel(row_ref, tile_ref, metric_ref, coeff_ref, support_ref, *refs):
-    out_ref, padded_out, picked_out, padded_ref, picked_ref, rows_ref, made_ref, *refs = refs
+def place_kernel(row_ref, metric_ref, coeff_ref, support_ref, padded_ref, picked_out, *refs):
+    picked_ref, item_ref, rows_ref, sem = refs
+    place(metric_ref, coeff_ref, support_ref, padded_ref, picked_ref, rows_ref)
+    for item in range(item_ref.shape[0]):
+        item_ref[item] = picked_ref[row_ref[item]]
+    copy = pltpu.make_async_copy(item_ref, picked_out.at[pl.ds(0, item_ref.shape[0])], sem)
+    copy.start()
+    copy.wait()
+
+
+def early_kernel(tile_ref, picked_in, out_ref, picked_ref, made_ref, *refs):
     buffer_ref, half_ref, slab_ref, sems = refs
     count = buffer_ref.shape[0]
     first = tile_ref.shape[0] - count
+    picked_copy = pltpu.make_async_copy(
+        picked_in.at[pl.ds(first, count)], picked_ref, sems.at[2 * count]
+    )
+    picked_copy.start()
     copies = fetch(tile_ref, first, buffer_ref, sems)
-    place(metric_ref, coeff_ref, support_ref, padded_ref, picked_ref, rows_ref)
-    placed = [
-        pltpu.make_async_copy(ref, out.at[pl.ds(0, ref.shape[0])], sems.at[2 * count + at])
-        for at, (ref, out) in enumerate(((padded_ref, padded_out), (picked_ref, picked_out)))
-    ]
-    for copy in placed:
-        copy.start()
+    picked_copy.wait()
     sends = [
         pltpu.make_async_copy(made_ref.at[item], out_ref.at[item], sems.at[count + item])
         for item in range(count)
@@ -120,12 +127,12 @@
         if at + rows.shape[0] == made_ref.shape[1]:
             sends[item].start()
 
-    half_tiles(row_ref, first, picked_ref, copies, buffer_ref, half_ref, slab_ref, put)
-    for copy in sends + placed:
+    half_tiles(picked_ref, copies, buffer_ref, half_ref, slab_ref, put)
+    for copy in sends:
         copy.wait()
 
 
-def late_kernel(row_ref, tile_ref, picked_in, out_ref, picked_ref, *refs):
+def late_kernel(tile_ref, picked_in, out_ref, picked_ref, *refs):
     buffer_ref, half_ref, slab_ref, sems = refs
     picked_copy = pltpu.make_async_copy(
         picked_in.at[pl.ds(0, picked_ref.shape[0])], picked_ref, sems.at[2 * buffer_ref.shape[0]]
@@ -137,13 +144,7 @@
     def put(item, at, rows):
         out_ref[item, at : at + rows.shape[0], :] = rows
 
-    half_tiles(row_ref, 0, picked_ref, copies, buffer_ref, half_ref, slab_ref, put)
-
-
-def stage_kernel(metric_in, metric_ref, sem):
-    copy = pltpu.make_async_copy(metric_in.at[pl.ds(0, metric_ref.shape[0])], metric_ref, sem)
-    copy.start()
-    copy.wait()
+    half_tiles(picked_ref, copies, buffer_ref, half_ref, slab_ref, put)
 
 
 def serve_kernel(asked_ref, metric_ref, out_ref):
@@ -282,36 +283,40 @@
 
     padded_shape = (metric.shape[0], depth, LANES)
     picked_shape = (support.shape[0], orbitals, width)
-    early, padded, picked = pl.pallas_call(
-        early_kernel,
+    padded, picked = pl.pallas_call(
+        place_kernel,
         out_shape=[
-            jax.ShapeDtypeStruct((early_count, late_rows, LANES), jnp.bfloat16),
-            jax.ShapeDtypeStruct((ROOM,) + padded_shape[1:], jnp.bfloat16),
+            jax.ShapeDtypeStruct(padded_shape, jnp.bfloat16),
             jax.ShapeDtypeStruct((ROOM,) + picked_shape[1:], jnp.bfloat16),
         ],
-        in_specs=[smem, anywhere, vmem, vmem, vmem],
-        out_specs=[anywhere] * 3,
+        in_specs=[smem] + [vmem] * 3,
+        out_specs=[vmem, anywhere],
         scratch_shapes=[
-            pltpu.VMEM(padded_shape, jnp.bfloat16),
             pltpu.VMEM(picked_shape, jnp.bfloat16),
+            pltpu.VMEM((item_count,) + picked_shape[1:], jnp.bfloat16),
             pltpu.VMEM((aux_width * metric.shape[0], LANES), jnp.float32),
+            pltpu.SemaphoreType.DMA,
+        ],
+        compiler_params=pltpu.CompilerParams(vmem_limit_bytes=EARLY_LIMIT),
+        name="place",
+    )(row_block, by_aux, coeff, support)
+
+    early = pl.pallas_call(
+        early_kernel,
+        out_shape=jax.ShapeDtypeStruct((early_count, late_rows, LANES), jnp.bfloat16),
+        in_specs=[anywhere, anywhere],
+        out_specs=anywhere,
+        scratch_shapes=[
+            pltpu.VMEM((early_count,) + picked_shape[1:], jnp.bfloat16),
             pltpu.VMEM((early_count, late_rows, LANES), jnp.bfloat16),
         ]
         + half_scratch(early_count),
-        compiler_params=pltpu.CompilerParams(vmem_limit_bytes=EARLY_LIMIT),
-        cost_estimate=cost(early_count),
+        compiler_params=pltpu.CompilerParams(vmem_limit_bytes=TILES_LIMIT),
+        cost_estimate=pl.CostEstimate(
+            flops=3 * 10**9, bytes_accessed=4 * 10**6, transcendentals=0
+        ),
         name="early",
-    )(row_block, tiles, by_aux, coeff, support)
-
-    padded = pl.pallas_call(
-        stage_kernel,
-        out_shape=jax.ShapeDtypeStruct(padded_shape, jnp.bfloat16),
-        in_specs=[anywhere],
-        out_specs=vmem,
-        scratch_shapes=[pltpu.SemaphoreType.DMA],
-        compiler_params=pltpu.CompilerParams(vmem_limit_bytes=STAGE_LIMIT),
-        name="stage",
-    )(padded)
+    )(tiles, picked)
 
     served = pl.pallas_call(
         serve_kernel,
@@ -327,13 +332,14 @@
     late = pl.pallas_call(
         late_kernel,
         out_shape=jax.ShapeDtypeStruct((late_count, late_rows, LANES), jnp.bfloat16),
-        in_specs=[smem, anywhere, anywhere],
+        in_specs=[anywhere, anywhere],
         out_specs=vmem,
-        scratch_shapes=[pltpu.VMEM(picked_shape, jnp.bfloat16)] + half_scratch(late_count),
+        scratch_shapes=[pltpu.VMEM((late_count,) + picked_shape[1:], jnp.bfloat16)]
+        + half_scratch(late_count),
         compiler_params=pltpu.CompilerParams(vmem_limit_bytes=LATE_LIMIT),
         cost_estimate=cost(late_count),
         name="late",
-    )(row_block, tiles, picked)
+    )(tiles, picked)
 
     cols = asked[:, 32 : 32 + item_count]
     late_steps, early_steps = (late_count + 1) // 2, (early_count + 1) // 2

time: 79.1 us -> 79.7 us (level)
    pallas_call x2, Pallas kernels: 5.73 us -> 6.9 us  [the longest x1 3.66 us: shards(): pl.pallas_call(early_kernel, out_shape=jax.ShapeDtypeStruct((early_count,...]
  transfers between devices with their start and end apart: 2 -> 2, of which waited for: 2 -> 1; matrix products, arithmetic and copies ran while one was open for 1% -> 1% of each run, Pallas kernels for 15% -> 16%
where the time goes in v9:
time: 79.7 us; the launch traced here: 79.4 us
  blocking collectives  42.7 us (54%)
  Pallas kernels  20.7 us (26%)
  starting transfers between devices  14.2 us (18%)
  waiting for transfers between devices  0.86 us (1%)
    all_to_all x1, blocking collectives, shards(): lax.all_to_all(sums.reshape(pair_count, rows, LANES), 'pair', split_axis=...  30.4 us
    all_to_all x1, blocking collectives, shards(): lax.all_to_all(blocks.reshape(aux_count, rows * SLOTS, LANES), 'aux', spl...  12.3 us
    all_to_all x1, starting transfers between devices, shards(): lax.all_to_all(request.reshape(aux_count, 1, LANES), 'aux', split_axis=0,...  7.58 us
    all_to_all x1, starting transfers between devices, shards(): lax.all_to_all(served, 'aux', split_axis=0, concat_axis=0, tiled=True)  6.65 us
    pallas_call x1, Pallas kernels, shards(): pl.pallas_call(late_kernel, out_shape=jax.ShapeDtypeStruct((late_count, l...  5.77 us
    pallas_call x2, Pallas kernels, terms(): pl.pallas_call(functools.partial(term_kernel, first, first_slot), out_sha...  4.14 us
    pallas_call x1, Pallas kernels, shards(): pl.pallas_call(early_kernel, out_shape=jax.ShapeDtypeStruct((early_count,...  3.66 us
    pallas_call x1, Pallas kernels, shards(): pl.pallas_call(place_kernel, out_shape=[jax.ShapeDtypeStruct(padded_shape...  3.24 us
  transfers between devices with their start and end apart: 2, of which 1 were waited for; matrix products, arithmetic and copies ran while one was open for 1% of the time, Pallas kernels for 16%

profile of v9, /device:TPU:1, one launch (start us, length us, event | category | flops | bytes accessed | tf_op | source)
XLA Modules:
  0.0 79.4 jit_solution(18178583814197001634)
XLA Ops:
  0.0 1.5 %request.1 = s32[16,128]{1,0:T(8,128)} custom-call(s32[1,11]{1,0:T(1,128)} %bitcast.19, s32[1,11]{1,0:T(1,128)} %bitcast.24, s32[1,11]{1,0:T(1,128)} %bitcast.25), custom_call_target="tpu_custom_call" | custom-call | tf_op jit(solution)/shard_map/request/pallas_call | solution.py:252
  1.5 7.6 %all-to-all-start = ((s32[16,1,128]{2,1,0:T(1,128)}), s32[16,1,128]{2,1,0:T(1,128)S(1)}, u32[]{:S(2)}, u32[]{:S(2)}) async-start(s32[16,1,128]{2,1,0:T(1,128)} %bitcast.23), calls=%async_computation | async-start | bytes 16384 | tf_op jit(solution)/shard_map/all_to_all | solution.py:259
  9.1 3.2 %place.1 = (bf16[32,56,128]{2,1,0:T(8,128)(2,1)}, bf16[700,48,64]{2,1,0:T(8,128)(2,1)}) custom-call(s32[11]{0:T(128)} %row_ref.1, bf16[52,32,52]{2,1,0:T(8,128)(2,1)} %bitcast.22, bf16[128,256]{1,0:T(8,128)(2,1)} %coeff_ref.1, s32[2,48]{1,0:T(2,128)} %support_ref.1), custom_call_target="tpu_custom_call" | custom-call | tf_op jit(solution)/shard_map/place/pallas_call | solution.py:286
  12.4 0.0 copy-start.1
  12.4 3.7 %early.1.halves_ref = bf16[3,1536,128]{2,1,0:T(8,128)(2,1)} custom-call(bf16[11,64,3328]{2,1,0:T(8,128)(2,1)} %tile_ref.3, bf16[700,48,64]{2,1,0:T(8,128)(2,1)} %get-tuple-element.12.picked_in), custom_call_target="tpu_custom_call" | custom-call | flops 3000000000 | bytes 4000000 | tf_op jit(solution)/shard_map/early/pallas_call | solution.py:304
  16.1 0.0 all-to-all-done
  16.1 0.1 fusion.9
  16.2 0.1 slice.22
  16.2 0.1 slice.24
  16.3 0.0 copy-done.1
  16.3 1.4 %serve.1 = bf16[16,56,128]{2,1,0:T(8,128)(2,1)} custom-call(s32[16,128]{1,0:T(8,128)S(1)} %bitcast.15, bf16[32,56,128]{2,1,0:T(8,128)(2,1)S(1)} %copy-done.1), custom_call_target="tpu_custom_call" | custom-call | tf_op jit(solution)/shard_map/serve/pallas_call | solution.py:321
  17.7 6.7 %all-to-all-start.1 = ((bf16[16,56,128]{2,1,0:T(8,128)(2,1)}), bf16[16,56,128]{2,1,0:T(8,128)(2,1)S(1)}, u32[]{:S(2)}, u32[]{:S(2)}) async-start(bf16[16,56,128]{2,1,0:T(8,128)(2,1)} %serve.1), calls=%async_computation.1 | async-start | bytes 458752 | tf_op jit(solution)/shard_map/all_to_all | solution.py:329
  24.4 0.1 select_add_fusion
  24.5 0.1 eq.59
  24.6 0.1 eq.63
  24.7 0.0 copy-start.2
  24.7 5.8 %late.1.halves_ref = bf16[8,1536,128]{2,1,0:T(8,128)(2,1)S(1)} custom-call(bf16[11,64,3328]{2,1,0:T(8,128)(2,1)} %tile_ref.3, bf16[700,48,64]{2,1,0:T(8,128)(2,1)} %get-tuple-element.12.picked_in), custom_call_target="tpu_custom_call" | custom-call | flops 163577856 | bytes 6553600 | tf_op jit(solution)/shard_map/late/pallas_call | solution.py:332
  30.5 0.2 select_convert_fusion.pick_ref
  30.7 0.9 %all-to-all-done.1.metric_ref = bf16[16,56,128]{2,1,0:T(8,128)(2,1)S(1)} async-done(((bf16[16,56,128]{2,1,0:T(8,128)(2,1)}), bf16[16,56,128]{2,1,0:T(8,128)(2,1)S(1)}, u32[]{:S(2)}, u32[]{:S(2)}) %all-to-all-start.1) | async-done | bytes 229408 | tf_op jit(solution)/shard_map/all_to_all | solution.py:329
  31.5 0.0 copy-done.2
  31.5 0.0 copy-start
  31.5 2.6 %late_term.1.refs_0_ = f32[512,128]{1,0:T(8,128)S(1)} custom-call(s32[11]{0:T(128)S(1)} %bitcast.20, bf16[8,1536,128]{2,1,0:T(8,128)(2,1)S(1)} %late.1.halves_ref, bf16[16,56,128]{2,1,0:T(8,128)(2,1)S(1)} %all-to-all-done.1.metric_ref), custom_call_target="tpu_custom_call" | custom-call | flops 3623878656 | bytes 3145728 | tf_op jit(solution)/shard_map/late_term/pallas_call | solution.py:370
  34.1 0.0 copy-done
  34.2 1.5 %early_term.1 = bf16[512,128]{1,0:T(8,128)(2,1)S(1)} custom-call(s32[11]{0:T(128)S(1)} %bitcast.21, bf16[3,1536,128]{2,1,0:T(8,128)(2,1)S(1)} %copy-done, bf16[16,56,128]{2,1,0:T(8,128)(2,1)S(1)} %all-to-all-done.1.metric_ref, f32[512,128]{1,0:T(8,128)S(1)} %late_term.1.refs_0_), custom_call_target="tpu_custom_call" | custom-call | flops 1358954496 | bytes 1179648 | tf_op jit(solution)/shard_map/early_term/pallas_call | solution.py:370
  35.7 12.3 %all_to_all.20.parts_ref = bf16[16,32,128]{2,1,0:T(8,128)(2,1)S(1)} all-to-all(bf16[16,32,128]{2,1,0:T(8,128)(2,1)S(1)} %bitcast.17), channel_id=1, replica_groups=mesh['pair'=32,'aux'=16] {'aux'}, dimensions={0} | all-to-all | bytes 262144 | tf_op jit(solution)/shard_map/all_to_all | solution.py:389
  48.0 0.3 combine.1
  48.3 30.4 %all_to_all.21 = bf16[32,4,128]{2,1,0:T(4,128)(2,1)S(1)} all-to-all(bf16[32,4,128]{2,1,0:T(4,128)(2,1)S(1)} %bitcast.16), channel_id=1, replica_groups=mesh['pair'=32,'aux'=16] {'pair'}, dimensions={0} | all-to-all | bytes 65536 | tf_op jit(solution)/shard_map/all_to_all | solution.py:402
  78.7 0.7 final.1
  (5 shorter events, 0.0 us)
Async XLA Ops:
  1.5 14.6 %all-to-all-start = ((s32[16,1,128]{2,1,0:T(1,128)}), s32[16,1,128]{2,1,0:T(1,128)S(1)}, u32[]{:S(2)}, u32[]{:S(2)}) async-start(s32[16,1,128]{2,1,0:T(1,128)} %bitcast.23), calls=%async_computation | async-start | bytes 16384 | tf_op jit(solution)/shard_map/all_to_all | solution.py:259
  12.4 3.9 %copy-start.1 = (bf16[32,56,128]{2,1,0:T(8,128)(2,1)S(1)}, bf16[32,56,128]{2,1,0:T(8,128)(2,1)}, u32[]{:S(2)}) copy-start(bf16[32,56,128]{2,1,0:T(8,128)(2,1)} %get-tuple-element.11.metric_ref) | copy-start | bytes 1376260
  17.7 13.8 %all-to-all-start.1 = ((bf16[16,56,128]{2,1,0:T(8,128)(2,1)}), bf16[16,56,128]{2,1,0:T(8,128)(2,1)S(1)}, u32[]{:S(2)}, u32[]{:S(2)}) async-start(bf16[16,56,128]{2,1,0:T(8,128)(2,1)} %serve.1), calls=%async_computation.1 | async-start | bytes 458752 | tf_op jit(solution)/shard_map/all_to_all | solution.py:329
  24.7 6.8 %copy-start.2 = (s32[11,1]{0,1:T(1,128)S(1)}, s32[11,1]{0,1:T(1,128)}, u32[]{:S(2)}) copy-start(s32[11,1]{0,1:T(1,128)} %param.13) | copy-start | bytes 136
  31.5 2.6 %copy-start = (bf16[3,1536,128]{2,1,0:T(8,128)(2,1)S(1)}, bf16[3,1536,128]{2,1,0:T(8,128)(2,1)}, u32[]{:S(2)}) copy-start(bf16[3,1536,128]{2,1,0:T(8,128)(2,1)} %early.1.halves_ref) | copy-start | bytes 3538948
